TPU v7x, 256 devices: a whole 4x4x8 slice. The times are simulated.
256 devices in a mesh: seq: 64 (over z, x, core), head: 4 (over y).
Axes of the slice: x: 4, y: 4, z: 8, core: 2. Of those that a mesh axis runs over, the one named last changes fastest.
Arguments:
- queries: bfloat16 [32768, 2048], P(('seq', 'head')), may hold values from -5 to 5
- keys: bfloat16 [32768, 2048], P(('seq', 'head')), may hold values from -5 to 5
- values: bfloat16 [32768, 2048], P(('seq', 'head')), may hold values from -6 to 6
- noise: bfloat16 [32768, 2048], P(('seq', 'head')), may hold values from -6 to 6
- random_blocks: int32 [512, 3], replicated, may hold values from 0 to 511, as said below
- global_blocks: int32 [2], replicated, may hold values from 0 to 511
Outputs:
- attended: bfloat16 [32768, 2048], P(('seq', 'head'))
- query_grad: bfloat16 [32768, 2048], P(('seq', 'head'))
- key_grad: bfloat16 [32768, 2048], P(('seq', 'head'))
- value_grad: bfloat16 [32768, 2048], P(('seq', 'head'))
Inputs may be any that keep to these rules, and one draw needn't show every extreme that they name: `random_blocks`: group the blocks into shards of 8 consecutive blocks. No query block names a random block of its own shard, and the 8 query blocks of one shard name together at most 1 random blocks of any one other shard, counting repeats; in every draw some shard names exactly 1 of some other shard.
All inputs are finite; a program needn't handle non-finite values.
Results may differ from a plain program's by a relative error of at most 0.033.
Values may be sent and summed in bfloat16 or wider, within the bound.
A program may use at most 128 MiB of HBM per device.

v0:
```python
import math

import jax
import jax.numpy as jnp
from jax import lax
from jax.sharding import PartitionSpec as P

DH = 128
BLK = 64


def extended(block, sides, width):
    for axis, dim in sides:
        count = lax.axis_size(axis)
        forward = [(i, i + 1) for i in range(count - 1)]
        backward = [(target, source) for source, target in forward]
        low = lax.ppermute(
            lax.slice_in_dim(block, block.shape[dim] - width, None, axis=dim), axis, forward
        )
        high = lax.ppermute(lax.slice_in_dim(block, 0, width, axis=dim), axis, backward)
        block = jnp.concatenate([low, block, high], axis=dim)
    return block


def broadcast(value, axis, source):
    kept = jnp.where(lax.axis_index(axis) == source, value, 0).astype(value.dtype)
    return lax.psum(kept, axis)


def shards(queries, keys, values, noise, random_blocks, global_blocks):
    scaling = 1.0 / math.sqrt(DH)
    q_all, k_all, v_all, n_all = (
        lax.all_to_all(queries, "head", split_axis=1, concat_axis=0, tiled=True),
        lax.all_to_all(keys, "head", split_axis=1, concat_axis=0, tiled=True),
        lax.all_to_all(values, "head", split_axis=1, concat_axis=0, tiled=True),
        lax.all_to_all(noise, "head", split_axis=1, concat_axis=0, tiled=True),
    )
    row_count, lane_width = q_all.shape
    head_count = lane_width // DH
    local_blocks = row_count // BLK
    seq_count = lax.axis_size("seq")
    seq_index = lax.axis_index("seq")
    pick_count = random_blocks.shape[1]
    glob_count = global_blocks.shape[0]
    key_count = 3 + pick_count + glob_count
    requests = local_blocks * pick_count
    slot_cap = (requests + seq_count - 2) // (seq_count - 1)
    slot_total = seq_count * slot_cap

    def to_heads(array):
        return array.reshape(local_blocks, BLK, head_count, DH).transpose(0, 2, 1, 3)

    def to_rows(array):
        return array.transpose(0, 2, 1, 3).reshape(row_count, lane_width)

    query_blocks = to_heads(q_all)
    noise_blocks = to_heads(n_all)
    key_value = jnp.stack([to_heads(k_all), to_heads(v_all)], 1)
    padded = extended(key_value, (("seq", 0),), 1)
    glob_owner = global_blocks // local_blocks
    glob_slot = global_blocks % local_blocks
    fetched = []
    for position in range(glob_count):
        one_piece = lax.dynamic_index_in_dim(key_value, glob_slot[position], 0, keepdims=False)
        fetched.append(broadcast(one_piece, "seq", glob_owner[position]))
    glob_pair = jnp.stack(fetched, 0)
    flat_req = random_blocks.reshape(seq_count, requests)
    req_owner = flat_req // local_blocks
    owners = jnp.arange(seq_count, dtype=jnp.int32)
    owner_hits = (req_owner[:, :, None] == owners[None, None, :]).astype(jnp.int32)
    slot_rank = jnp.sum((jnp.cumsum(owner_hits, axis=1) - 1) * owner_hits, axis=2)
    own_requests = lax.dynamic_index_in_dim(flat_req, seq_index, 0, keepdims=False)
    own_rank = lax.dynamic_index_in_dim(slot_rank, seq_index, 0, keepdims=False)
    slot_of = own_requests // local_blocks * slot_cap + own_rank
    slot_ids = jnp.arange(slot_cap, dtype=jnp.int32)
    matches = (
        (req_owner == seq_index)[:, :, None] & (slot_rank[:, :, None] == slot_ids[None, None, :])
    ).astype(jnp.int32)
    send_index = jnp.sum(matches * (flat_req % local_blocks)[:, :, None], axis=1).reshape(-1)
    send_valid = (jnp.sum(matches, axis=1) > 0).reshape(-1)
    outgoing = jnp.take(key_value, send_index, axis=0)
    incoming = lax.all_to_all(outgoing, "seq", split_axis=0, concat_axis=0, tiled=True)
    rand_pair = jnp.take(incoming, slot_of, axis=0).reshape(
        local_blocks, pick_count, 2, head_count, BLK, DH
    )
    window = jnp.stack([padded[:-2], padded[1:-1], padded[2:]], 1)
    glob_all = jnp.broadcast_to(glob_pair[None], (local_blocks, glob_count, 2, head_count, BLK, DH))
    all_pairs = jnp.concatenate([window, rand_pair, glob_all], 1)
    key_blocks = (
        all_pairs[:, :, 0]
        .transpose(0, 2, 1, 3, 4)
        .reshape(local_blocks, head_count, key_count * BLK, DH)
    )
    value_blocks = (
        all_pairs[:, :, 1]
        .transpose(0, 2, 1, 3, 4)
        .reshape(local_blocks, head_count, key_count * BLK, DH)
    )
    block_ids = seq_index * local_blocks + jnp.arange(local_blocks, dtype=jnp.int32)
    block_total = local_blocks * seq_count
    present = jnp.concatenate(
        [
            (block_ids >= 1)[:, None],
            jnp.ones((local_blocks, 1), jnp.bool_),
            (block_ids + 1 < block_total)[:, None],
            jnp.ones((local_blocks, pick_count + glob_count), jnp.bool_),
        ],
        1,
    )
    present_rows = jnp.repeat(present, BLK, axis=1)
    scores = (
        jnp.einsum("ihad,ihkd->ihak", query_blocks, key_blocks, preferred_element_type=jnp.float32)
        * scaling
    )
    scores = jnp.where(present_rows[:, None, None, :], scores, -jnp.inf)
    row_max = jnp.max(scores, axis=3, keepdims=True)
    weights_raw = jnp.exp(scores - row_max)
    row_sum = jnp.sum(weights_raw, axis=3, keepdims=True)
    probs_full = weights_raw / row_sum
    probs_bf = probs_full.astype(jnp.bfloat16)
    attended = jnp.einsum(
        "ihak,ihkd->ihad", probs_bf, value_blocks, preferred_element_type=jnp.float32
    ).astype(jnp.bfloat16)
    out_grad = (attended.astype(jnp.float32) - noise_blocks.astype(jnp.float32)).astype(
        jnp.bfloat16
    )
    dprobs = jnp.einsum(
        "ihad,ihkd->ihak", out_grad, value_blocks, preferred_element_type=jnp.float32
    )
    delta_row = jnp.sum(probs_full * dprobs, axis=3, keepdims=True)
    dscores = (probs_full * (dprobs - delta_row)).astype(jnp.bfloat16)
    query_grad = (
        jnp.einsum("ihak,ihkd->ihad", dscores, key_blocks, preferred_element_type=jnp.float32)
        * scaling
    ).astype(jnp.bfloat16)

    def block_terms(first_key, last_key):
        span = last_key - first_key
        key_part = (
            jnp.einsum(
                "ihak,ihad->ihkd",
                dscores[:, :, :, first_key * BLK : last_key * BLK],
                query_blocks,
                preferred_element_type=jnp.float32,
            )
            * scaling
        )
        value_part = jnp.einsum(
            "ihak,ihad->ihkd",
            probs_bf[:, :, :, first_key * BLK : last_key * BLK],
            out_grad,
            preferred_element_type=jnp.float32,
        )
        key_part = key_part.reshape(local_blocks, head_count, span, BLK, DH).transpose(
            0, 2, 1, 3, 4
        )
        value_part = value_part.reshape(local_blocks, head_count, span, BLK, DH).transpose(
            0, 2, 1, 3, 4
        )
        return jnp.stack([key_part, value_part], 2)

    no_pad = ((0, 0),) * 4
    window_terms = block_terms(0, 3)
    local_grads = window_terms[:, 1]
    local_grads = local_grads + jnp.pad(window_terms[1:, 0], ((0, 1),) + no_pad)
    local_grads = local_grads + jnp.pad(window_terms[:-1, 2], ((1, 0),) + no_pad)
    edge_grads = jnp.stack([window_terms[0, 0], window_terms[local_blocks - 1, 2]], 0)
    arrived = extended(edge_grads.astype(jnp.bfloat16), (("seq", 0),), 1).astype(edge_grads.dtype)
    local_grads = local_grads.at[0].add(arrived[0]).at[local_blocks - 1].add(arrived[3])
    glob_terms = jnp.sum(block_terms(3 + pick_count, key_count), axis=0)
    glob_sum = lax.psum(glob_terms, "seq")
    glob_owned = (glob_owner == seq_index)[:, None, None, None, None]
    local_grads = local_grads.at[glob_slot].add(jnp.where(glob_owned, glob_sum, 0.0))
    valid_mask = send_valid[:, None, None, None, None]
    rand_terms = (
        block_terms(3, 3 + pick_count)
        .astype(jnp.bfloat16)
        .reshape(requests, 2, head_count, BLK, DH)
    )
    grads_out = (
        jnp.zeros((slot_total, 2, head_count, BLK, DH), jnp.bfloat16).at[slot_of].set(rand_terms)
    )
    returned = lax.all_to_all(grads_out, "seq", split_axis=0, concat_axis=0, tiled=True)
    local_grads = local_grads.at[send_index].add(
        jnp.where(valid_mask, returned.astype(jnp.float32), 0.0)
    )
    key_grad = to_rows(local_grads[:, 0]).astype(jnp.bfloat16)
    value_grad = to_rows(local_grads[:, 1]).astype(jnp.bfloat16)
    return (
        lax.all_to_all(to_rows(attended), "head", split_axis=0, concat_axis=1, tiled=True),
        lax.all_to_all(to_rows(query_grad), "head", split_axis=0, concat_axis=1, tiled=True),
        lax.all_to_all(key_grad, "head", split_axis=0, concat_axis=1, tiled=True),
        lax.all_to_all(value_grad, "head", split_axis=0, concat_axis=1, tiled=True),
    )


def solution(mesh):
    return jax.shard_map(
        shards,
        mesh=mesh,
        in_specs=(
            P(("seq", "head"), None),
            P(("seq", "head"), None),
            P(("seq", "head"), None),
            P(("seq", "head"), None),
            P(),
            P(),
        ),
        out_specs=(
            P(("seq", "head"), None),
            P(("seq", "head"), None),
            P(("seq", "head"), None),
            P(("seq", "head"), None),
        ),
        check_vma=False,
    )
```

profile of v0, /device:TPU:8, one launch (start us, length us, event | category | flops | bytes accessed | tf_op | source)
XLA Modules:
  0.0 727.3 jit_solution(15165887073139953883)
XLA Ops:
  9.2 5.6 all-to-all-start
  25.2 4.8 all-to-all-start.1
  33.0 3.8 all-to-all-done.1
  36.7 4.9 all-to-all-start.3
  49.1 3.9 pad_maximum_fusion.2
  53.1 9.4 %gather_fusion = bf16[64,2,4,64,128]{4,2,3,1,0:T(4,128)(2,1)} fusion(bf16[8,2,4,64,128]{4,2,3,0,1:T(4,128)(2,1)S(1)} %get-tuple-element.60, s32[1024]{0:T(1024)S(1)} %pad_clamp_fusion.1), kind=kCustom, calls=%fused_computation | custom fusion | bytes 16777472 | tf_op jit(solution)/shard_map/jit(_take)/gather | solution.py:81
  62.4 4.8 all-to-all-start.5
  67.2 8.5 %broadcast_select_fusion = bf16[64,2,4,64,128]{4,2,3,1,0:T(4,128)(2,1)} fusion(bf16[64,2,4,64,128]{4,2,3,1,0:T(4,128)(2,1)} %gather_fusion, pred[64]{0:T(512)(128)(4,1)S(1)} %compare_and_fusion.1), kind=kLoop, calls=%fused_computation.14 | loop fusion | flops 4194304 | bytes 16777280 | tf_op jit(solution)/shard_map/jit(_take)/select_n | solution.py:81
  75.8 16.8 %all-to-all-start.2 = ((bf16[64,2,4,64,128]{4,2,3,1,0:T(4,128)(2,1)}), bf16[64,2,4,64,128]{4,2,3,1,0:T(4,128)(2,1)}, u32[]{:S(2)}, u32[]{:S(2)}) async-start(bf16[64,2,4,64,128]{4,2,3,1,0:T(4,128)(2,1)} %broadcast_select_fusion), calls=%async_computation.2 | async-start | bytes 16777216 | tf_op jit(solution)/shard_map/all_to_all | solution.py:82
  95.6 231.5 %all-reduce.8.cloned.1.call-done = (bf16[1,2,4,64,128]{4,2,3,0,1:T(4,128)(2,1)}, bf16[1,2,4,64,128]{4,2,3,0,1:T(4,128)(2,1)}) async-done(((bf16[1,2,4,64,128]{4,2,3,0,1:T(4,128)(2,1)}, bf16[1,2,4,64,128]{4,2,3,0,1:T(4,128)(2,1)}), (bf16[1,2,4,64,128]{4,2,3,0,1:T(4,128)(2,1)}, bf16[1,2,4,64,128]{4,2,3,0,1:T(4,128)(2,1)})) %all-reduce.8.cloned.1.call-update) | async-done | bytes 262160 | tf_op jit(solution)/shard_map/psum | solution.py:27
  333.3 8.8 %gather_fusion.1 = bf16[24,2,4,64,128]{4,2,3,1,0:T(4,128)(2,1)} fusion(bf16[64,2,4,64,128]{4,2,3,1,0:T(4,128)(2,1)} %all-to-all-done.2, s32[1024]{0:T(1024)S(1)} %pad_clamp_fusion), kind=kCustom, calls=%fused_computation.1 | custom fusion | bytes 6291552 | tf_op jit(solution)/shard_map/jit(_take)/gather | solution.py:83
  349.6 4.5 slice_bitcast_fusion
  365.6 5.0 all-to-all-start.4
  370.6 5.3 multiply_reduce_fusion
  382.4 5.4 broadcast_in_dim.109
  387.7 8.7 %scatter_fusion.1 = bf16[64,2,4,64,128]{4,3,2,1,0:T(8,128)(2,1)} fusion(bf16[64,2,4,64,128]{4,3,2,1,0:T(8,128)(2,1)} %broadcast_in_dim.109, s32[24]{0:T(128)S(1)} %fusion.62, bf16[24,2,4,64,128]{4,3,2,1,0:T(8,128)(2,1)} %pad_maximum_fusion.1), kind=kCustom, calls=%fused_computation.3 | custom fusion | bytes 9437280 | tf_op jit(solution)/shard_map/scatter | solution.py:181
  396.4 8.2 %all-to-all-start.7 = ((bf16[64,2,4,64,128]{4,3,2,1,0:T(8,128)(2,1)}), bf16[64,2,4,64,128]{4,3,2,1,0:T(8,128)(2,1)}, u32[]{:S(2)}, u32[]{:S(2)}) async-start(bf16[64,2,4,64,128]{4,3,2,1,0:T(8,128)(2,1)} %scatter_fusion.1), calls=%async_computation.7 | async-start | bytes 16777216 | tf_op jit(solution)/shard_map/all_to_all | solution.py:183
  425.3 227.1 %all-reduce.6.cloned.1.call-done = f32[2,2,4,64,128]{4,3,0,2,1:T(8,128)} async-done(((f32[2,2,4,64,128]{4,3,0,2,1:T(8,128)}), f32[2,2,4,64,128]{4,3,0,2,1:T(8,128)}) %all-reduce.6.cloned.1.call-update) | async-done | bytes 524304 | tf_op jit(solution)/shard_map/psum | solution.py:171
  654.5 4.8 all-to-all-start.6
  659.3 12.2 %convert_select_fusion = f32[64,2,4,64,128]{4,3,2,1,0:T(8,128)} fusion(bf16[64,2,4,64,128]{4,3,2,1,0:T(8,128)(2,1)} %all-to-all-done.7, pred[64]{0:T(512)(128)(4,1)S(1)} %broadcast_compare_fusion.3), kind=kLoop, calls=%fused_computation.6 | loop fusion | flops 8388608 | bytes 25165888 | tf_op jit(solution)/shard_map/jit(_where)/select_n | solution.py:185
  671.5 22.8 %scatter_fusion.2 = f32[8,2,4,64,128]{4,3,2,1,0:T(8,128)S(1)} fusion(f32[8,2,4,64,128]{4,3,2,1,0:T(8,128)S(1)} %scatter_fusion, s32[64]{0:T(128)S(1)} %fusion.61, f32[64,2,4,64,128]{4,3,2,1,0:T(8,128)} %convert_select_fusion), kind=kCustom, calls=%fused_computation.4 | custom fusion | flops 4194304 | bytes 50331904 | tf_op jit(solution)/shard_map/scatter-add | solution.py:184
  696.0 4.8 all-to-all-start.9
  702.2 5.2 all-to-all-done.9
  707.4 4.9 all-to-all-start.8
  (156 shorter events, 85.6 us)
Async XLA Ops:
  7.2 17.2 %copy-start.15 = (bf16[128,2048]{1,0:T(8,128)(2,1)S(1)}, bf16[128,2048]{1,0:T(8,128)(2,1)}, u32[]{:S(2)}) copy-start(bf16[128,2048]{1,0:T(8,128)(2,1)} %param.12) | copy-start | bytes 1572868
  7.2 23.5 %copy-start.16 = (bf16[128,2048]{1,0:T(8,128)(2,1)S(1)}, bf16[128,2048]{1,0:T(8,128)(2,1)}, u32[]{:S(2)}) copy-start(bf16[128,2048]{1,0:T(8,128)(2,1)} %param.10) | copy-start | bytes 1572868
  9.2 16.1 %all-to-all-start = ((bf16[128,4,512]{2,0,1:T(8,128)(2,1)}), bf16[128,4,512]{2,0,1:T(8,128)(2,1)S(1)}, u32[]{:S(2)}, u32[]{:S(2)}) async-start(bf16[128,4,512]{2,0,1:T(8,128)(2,1)} %bitcast.167), calls=%async_computation | async-start | bytes 1048576 | tf_op jit(solution)/shard_map/all_to_all | solution.py:34
  25.2 11.5 %all-to-all-start.1 = ((bf16[128,4,512]{2,0,1:T(8,128)(2,1)}), bf16[128,4,512]{2,0,1:T(8,128)(2,1)S(1)}, u32[]{:S(2)}, u32[]{:S(2)}) async-start(bf16[128,4,512]{2,0,1:T(8,128)(2,1)} %bitcast.166), calls=%async_computation.1 | async-start | bytes 1048576 | tf_op jit(solution)/shard_map/all_to_all | solution.py:35
  36.7 25.7 %all-to-all-start.3 = ((bf16[128,4,512]{2,0,1:T(8,128)(2,1)}), bf16[128,4,512]{2,0,1:T(8,128)(2,1)S(1)}, u32[]{:S(2)}, u32[]{:S(2)}) async-start(bf16[128,4,512]{2,0,1:T(8,128)(2,1)} %bitcast.165), calls=%async_computation.3 | async-start | bytes 1048576 | tf_op jit(solution)/shard_map/all_to_all | solution.py:33
  42.9 4.5 collective-permute-start
  44.2 5.0 collective-permute-start.1
  62.4 13.3 %all-to-all-start.5 = ((bf16[128,4,512]{2,0,1:T(8,128)(2,1)}), bf16[128,4,512]{2,0,1:T(8,128)(2,1)S(1)}, u32[]{:S(2)}, u32[]{:S(2)}) async-start(bf16[128,4,512]{2,0,1:T(8,128)(2,1)} %bitcast.164), calls=%async_computation.5 | async-start | bytes 1048576 | tf_op jit(solution)/shard_map/all_to_all | solution.py:36
  75.8 257.5 %all-to-all-start.2 = ((bf16[64,2,4,64,128]{4,2,3,1,0:T(4,128)(2,1)}), bf16[64,2,4,64,128]{4,2,3,1,0:T(4,128)(2,1)}, u32[]{:S(2)}, u32[]{:S(2)}) async-start(bf16[64,2,4,64,128]{4,2,3,1,0:T(4,128)(2,1)} %broadcast_select_fusion), calls=%async_computation.2 | async-start | bytes 16777216 | tf_op jit(solution)/shard_map/all_to_all | solution.py:82
  92.6 234.5 %all-reduce.8.cloned.1.call-start = ((), (), s32[]{:S(2)}) async-start(), calls=%async_computation.11 | async-start | bytes 524288 | tf_op jit(solution)/shard_map/psum | solution.py:27
  94.1 236.6 %copy-start.13 = (bf16[8,1,2,4,64,128]{5,3,4,0,2,1:T(4,128)(2,1)S(1)}, bf16[8,1,2,4,64,128]{5,3,4,0,2,1:T(4,128)(2,1)}, u32[]{:S(2)}) copy-start(bf16[8,1,2,4,64,128]{5,3,4,0,2,1:T(4,128)(2,1)} %get-tuple-element.61) | copy-start | bytes 3145732
  94.3 315.1 %copy-start.8 = (bf16[8,64,4,128]{3,2,1,0:T(4,128)(2,1)}, bf16[8,64,4,128]{3,2,1,0:T(4,128)(2,1)S(1)}, u32[]{:S(2)}) copy-start(bf16[8,64,4,128]{3,2,1,0:T(4,128)(2,1)S(1)} %reshape.378) | copy-start | bytes 1572868
  95.6 236.4 %copy-start.12 = (bf16[8,1,2,4,64,128]{5,3,4,0,2,1:T(4,128)(2,1)S(1)}, bf16[8,1,2,4,64,128]{5,3,4,0,2,1:T(4,128)(2,1)}, u32[]{:S(2)}) copy-start(bf16[8,1,2,4,64,128]{5,3,4,0,2,1:T(4,128)(2,1)} %get-tuple-element.62) | copy-start | bytes 3145732
  364.2 13.9 %copy-start.10 = (bf16[8,4,64,128]{3,2,1,0:T(8,128)(2,1)}, bf16[8,4,64,128]{3,2,1,0:T(8,128)(2,1)S(1)}, u32[]{:S(2)}) copy-start(bf16[8,4,64,128]{3,2,1,0:T(8,128)(2,1)S(1)} %get-tuple-element.70) | copy-start | bytes 1572868
  365.6 30.8 %all-to-all-start.4 = ((bf16[4,128,512]{2,1,0:T(8,128)(2,1)}), bf16[4,128,512]{2,1,0:T(8,128)(2,1)}, u32[]{:S(2)}, u32[]{:S(2)}) async-start(bf16[4,128,512]{2,1,0:T(8,128)(2,1)} %all_to_all.114), calls=%async_computation.4 | async-start | bytes 1048576 | tf_op jit(solution)/shard_map/all_to_all | solution.py:190
  376.7 32.7 %copy-start.2 = (bf16[8,4,64,512]{3,2,1,0:T(8,128)(2,1)}, bf16[8,4,64,512]{3,2,1,0:T(8,128)(2,1)S(1)}, u32[]{:S(2)}) copy-start(bf16[8,4,64,512]{3,2,1,0:T(8,128)(2,1)S(1)} %multiply_convert_fusion) | copy-start | bytes 6291460
  396.4 258.1 %all-to-all-start.7 = ((bf16[64,2,4,64,128]{4,3,2,1,0:T(8,128)(2,1)}), bf16[64,2,4,64,128]{4,3,2,1,0:T(8,128)(2,1)}, u32[]{:S(2)}, u32[]{:S(2)}) async-start(bf16[64,2,4,64,128]{4,3,2,1,0:T(8,128)(2,1)} %scatter_fusion.1), calls=%async_computation.7 | async-start | bytes 16777216 | tf_op jit(solution)/shard_map/all_to_all | solution.py:183
  404.6 247.8 %all-reduce.6.cloned.1.call-start = ((), (), s32[]{:S(2)}) async-start(), calls=%async_computation.10 | async-start | bytes 1048576 | tf_op jit(solution)/shard_map/psum | solution.py:171
  411.1 11.0 %copy-start.1 = (f32[8,4,3,64,128]{4,3,1,0,2:T(8,128)}, f32[8,4,3,64,128]{4,3,1,0,2:T(8,128)S(1)}, u32[]{:S(2)}) copy-start(f32[8,4,3,64,128]{4,3,1,0,2:T(8,128)S(1)} %copy.224) | copy-start | bytes 9437188
  418.7 5.7 collective-permute-start.2
  420.8 4.4 collective-permute-start.3
  654.5 41.5 %all-to-all-start.6 = ((bf16[4,128,512]{2,1,0:T(8,128)(2,1)}), bf16[4,128,512]{2,1,0:T(8,128)(2,1)S(1)}, u32[]{:S(2)}, u32[]{:S(2)}) async-start(bf16[4,128,512]{2,1,0:T(8,128)(2,1)} %all_to_all.120), calls=%async_computation.6 | async-start | bytes 1048576 | tf_op jit(solution)/shard_map/all_to_all | solution.py:191
  696.0 11.4 %all-to-all-start.9 = ((bf16[4,128,512]{2,1,0:T(8,128)(2,1)}), bf16[4,128,512]{2,1,0:T(8,128)(2,1)S(1)}, u32[]{:S(2)}, u32[]{:S(2)}) async-start(bf16[4,128,512]{2,1,0:T(8,128)(2,1)} %convert_element_type.106), calls=%async_computation.9 | async-start | bytes 1048576 | tf_op jit(solution)/shard_map/all_to_all | solution.py:193
  707.4 11.5 %all-to-all-start.8 = ((bf16[4,128,512]{2,1,0:T(8,128)(2,1)}), bf16[4,128,512]{2,1,0:T(8,128)(2,1)S(1)}, u32[]{:S(2)}, u32[]{:S(2)}) async-start(bf16[4,128,512]{2,1,0:T(8,128)(2,1)} %convert_element_type.103), calls=%async_computation.8 | async-start | bytes 1048576 | tf_op jit(solution)/shard_map/all_to_all | solution.py:192
  (9 other events, 25.3 us)
Sparse Core Ops, SparseCore 0:
  97.6 229.4 all-reduce.7
  416.0 236.3 all-reduce.5
where the time goes:
time: 737 us; the launch traced here: 727 us
  waiting for transfers between devices  472 us (64%)
  local copies, waits for them, and re-layouts  76.7 us (10%)
  starting transfers between devices  71.1 us (10%)
  other arithmetic  67.8 us (9%)
  between operations  20.1 us (3%)
  matrix products  19.6 us (3%)
    psum x1, waiting for transfers between devices, broadcast(): return lax.psum(kept, axis)  231 us
    psum x1, waiting for transfers between devices, shards(): glob_sum = lax.psum(glob_terms, 'seq')  227 us
    scatter-add x1, other arithmetic, shards(): local_grads.at[send_index]  22.8 us
    all_to_all x1, starting transfers between devices, shards(): lax.all_to_all(outgoing, 'seq', split_axis=0, concat_axis=0, tiled=True)  16.8 us
  transfers between devices with their start and end apart: 16, of which 7 were waited for; matrix products, arithmetic and copies ran while one was open for 17% of the time, Pallas kernels for 0%

commit v1 on v0

v1 whole, which is shorter than its diff:
```python
import functools
import math

import jax
import jax.numpy as jnp
from jax import lax
from jax.experimental import pallas as pl
from jax.experimental.pallas import tpu as pltpu
from jax.sharding import PartitionSpec as P

DH = 128
BLK = 64
NX, NY, NZ, NC = 4, 4, 8, 2
ROWS = 128
SHARD = NY * ROWS
PER = SHARD // BLK
NB = NZ * NX * NC * PER
QUERIES = NX * PER
ENTRIES = 8
GROUP = 4
MESH = pl.DeviceIdType.MESH
STEPS = ((4, 3), (3, 4))


def place():
    seq, y = lax.axis_index("seq"), lax.axis_index("head")
    return seq // (NX * NC), (seq // NC) % NX, y, seq % NC


def device(z, x, y, c):
    return ((z * NX + x) * NC + c, y)


def around(base, step, count):
    return (base + step + count) % count


def greet(z, x, y, c):
    barrier = pltpu.get_barrier_semaphore()

    def signal(target):
        pl.semaphore_signal(barrier, inc=1, device_id=target, device_id_type=MESH)

    def plane(p, carry):
        signal(device(z, (x + p // NY) % NX, (y + p % NY) % NY, c))
        return carry

    lax.fori_loop(1, NX * NY, plane, 0)
    signal(device((z + 1) % NZ, x, y, c))
    signal(device((z + NZ - 1) % NZ, x, y, c))
    signal(device(z, x, y, 1 - c))
    pl.semaphore_wait(barrier, NX * NY - 1 + 3)


def remote(src, dst, send, recv, target):
    return pltpu.make_async_remote_copy(
        src_ref=src, dst_ref=dst, send_sem=send, recv_sem=recv, device_id=target, device_id_type=MESH
    )


def fetch_kernel(
    q, k, v, n, q_out, n_out, kv,
    plane_send, plane_recv, own_sem, ring_send, ring_recv, pair_send, pair_recv,
):
    z, x, y, c = place()
    greet(z, x, y, c)

    def columns(h):
        return pl.ds(pl.multiple_of(h * DH, DH), DH)

    def rows(at):
        return pl.ds(pl.multiple_of(at * ROWS, ROWS), ROWS)

    def landing(a, xs, ys):
        if a < 2:
            return kv.at[a, z, xs, c, rows(ys)]
        return (q_out, n_out)[a - 2].at[xs, rows(ys)]

    sources = (k, v, q, n)

    def tile_out(a, p):
        px, py = (x + p // NY) % NX, (y + p % NY) % NY
        return remote(
            sources[a].at[:, columns(px * NY + py)], landing(a, x, y),
            plane_send.at[a, p], plane_recv.at[a, p], device(z, px, py, c),
        )

    def tile_in(a, p):
        px, py = (x + NX - p // NY) % NX, (y + NY - p % NY) % NY
        return remote(
            sources[a].at[:, columns(px * NY + py)], landing(a, px, py),
            plane_send.at[a, p], plane_recv.at[a, p], device(z, px, py, c),
        )

    def tile_own(a):
        return pltpu.make_async_copy(
            sources[a].at[:, columns(x * NY + y)], landing(a, x, y), own_sem.at[a]
        )

    for a in range(4):
        tile_own(a).start()
    for first in (0, 2):
        def start(p, carry):
            tile_out(first, p).start()
            tile_out(first + 1, p).start()
            return carry

        lax.fori_loop(1, NX * NY, start, 0)

    def ring(a, way, step, j):
        sign = 1 if way == 0 else -1
        chunk = kv.at[a, around(z, -sign * (step - 1), NZ), around(x, -j, NX), c]
        return remote(
            chunk, chunk, ring_send.at[a, way, step - 1, j], ring_recv.at[a, way, step - 1, j],
            device(around(z, sign, NZ), x, y, c),
        )

    def ring_in(a, way, step, j):
        sign = 1 if way == 0 else -1
        chunk = kv.at[a, around(z, -sign * step, NZ), around(x, -j, NX), c]
        return remote(
            chunk, chunk, ring_send.at[a, way, step - 1, j], ring_recv.at[a, way, step - 1, j],
            device(around(z, -sign, NZ), x, y, c),
        )

    def pair(a, off, j, core):
        chunk = kv.at[a, around(z, off, NZ), around(x, -j, NX), core]
        return remote(
            chunk, chunk, pair_send.at[a, off + 4, j], pair_recv.at[a, off + 4, j],
            device(z, x, y, 1 - c),
        )

    def offsets(a):
        right, left = STEPS[a]
        return range(-right, left + 1)

    for step in range(1, 6):
        def chunk_step(j, carry):
            for a in range(2):
                if step == 1:
                    for dy in range(NY):
                        if dy == 0:
                            @pl.when(j == 0)
                            def _():
                                tile_own(a).wait()

                            @pl.when(j > 0)
                            def _():
                                tile_in(a, j * NY).wait_recv()
                        else:
                            tile_in(a, j * NY + dy).wait_recv()
                for way in range(2):
                    count = STEPS[a][way]
                    if 1 < step <= count + 1:
                        ring_in(a, way, step - 1, j).wait_recv()
                    if step <= count:
                        ring(a, way, step, j).start()
                    if 1 < step <= count + 1:
                        pair(a, (step - 1) * (-1 if way == 0 else 1), j, c).start()
                if step == 1:
                    pair(a, 0, j, c).start()
            return carry

        lax.fori_loop(0, NX, chunk_step, 0)

    for a in (2, 3):
        tile_own(a).wait()

    def finish_plane(p, carry):
        for a in range(4):
            tile_out(a, p).wait_send()
            if a >= 2:
                tile_in(a, p).wait_recv()
        return carry

    lax.fori_loop(1, NX * NY, finish_plane, 0)

    def finish_chunks(j, carry):
        for a in range(2):
            for way in range(2):
                for step in range(1, STEPS[a][way] + 1):
                    ring(a, way, step, j).wait_send()
            for off in offsets(a):
                pair(a, off, j, c).wait_send()
                pair(a, off, j, 1 - c).wait_recv()
        return carry

    lax.fori_loop(0, NX, finish_chunks, 0)


def attend_kernel(
    lists, firsts, q, n, kv_hbm, att, dq, part, kv, acc, load_sem, store_sem,
):
    scaling = 1.0 / math.sqrt(DH)
    loads = [pltpu.make_async_copy(kv_hbm.at[a], kv.at[a], load_sem.at[a]) for a in range(2)]
    for load in loads:
        load.start()

    def clear(i, carry):
        for a in range(2):
            acc[a, pl.ds(i * 8, 8)] = jnp.zeros((8, BLK, DH), jnp.float32)
        return carry

    lax.fori_loop(0, NB // 8, clear, 0)
    for load in loads:
        load.wait()

    column = lax.broadcasted_iota(jnp.int32, (1, ENTRIES * BLK), 1) // BLK

    def dot(a, b, dims):
        return lax.dot_general(a, b, (dims, ((), ())), preferred_element_type=jnp.float32)

    def group(g, carry):
        ids = [g * GROUP + u for u in range(GROUP)]
        entries = [[lists[i, e] for e in range(ENTRIES)] for i in ids]
        qs = [q[i] for i in ids]
        ks = [jnp.concatenate([kv[0, e] for e in es], 0) for es in entries]
        scores = [dot(a, b, ((1,), (1,))) * scaling for a, b in zip(qs, ks)]
        masked = []
        for i, s in zip(ids, scores):
            block = firsts[i]
            gone = ((column == 0) & (block == 0)) | ((column == 2) & (block == NB - 1))
            masked.append(jnp.where(gone, -jnp.inf, s))
        raws = [jnp.exp(s - jnp.max(s, 1, keepdims=True)) for s in masked]
        probs = [r * (1.0 / jnp.sum(r, 1, keepdims=True)) for r in raws]
        probs_bf = [p.astype(jnp.bfloat16) for p in probs]
        vs = [jnp.concatenate([kv[1, e] for e in es], 0) for es in entries]
        atts = [dot(p, b, ((1,), (0,))).astype(jnp.bfloat16) for p, b in zip(probs_bf, vs)]
        grads = []
        for i, a in zip(ids, atts):
            att[i] = a
            grads.append((a.astype(jnp.float32) - n[i].astype(jnp.float32)).astype(jnp.bfloat16))
        dprobs = [dot(d, b, ((1,), (1,))) for d, b in zip(grads, vs)]
        dscores = [
            (p * (d - jnp.sum(p * d, 1, keepdims=True))).astype(jnp.bfloat16)
            for p, d in zip(probs, dprobs)
        ]
        for i, d, b in zip(ids, dscores, ks):
            dq[i] = (dot(d, b, ((1,), (0,))) * scaling).astype(jnp.bfloat16)
        dks = [dot(d, a, ((0,), (0,))) * scaling for d, a in zip(dscores, qs)]
        dvs = [dot(p, d, ((0,), (0,))) for p, d in zip(probs_bf, grads)]
        for es, dk, dv in zip(entries, dks, dvs):
            for e in range(ENTRIES):
                acc[0, es[e]] += dk[e * BLK : (e + 1) * BLK]
                acc[1, es[e]] += dv[e * BLK : (e + 1) * BLK]
        return carry

    lax.fori_loop(0, QUERIES // GROUP, group, 0)

    def store(a, i):
        span = pl.ds(i * 64, 64)
        return pltpu.make_async_copy(kv.at[a, span], part.at[a, span], store_sem.at[a, i])

    for a in range(2):
        def out(i, carry):
            def cast(s, inner):
                at = pl.ds(i * 64 + s * 8, 8)
                kv[a, at] = acc[a, at].astype(jnp.bfloat16)
                return inner

            lax.fori_loop(0, 8, cast, 0)
            store(a, i).start()
            return carry

        lax.fori_loop(0, NB // 64, out, 0)
    for a in range(2):
        def done(i, carry):
            store(a, i).wait()
            return carry

        lax.fori_loop(0, NB // 64, done, 0)


def return_kernel(
    att, dq, part, att_out, dq_out, dk_out, dv_out,
    own, sib, came, own_sem, pair_send, pair_recv, ring_send, ring_recv,
    plane_send, plane_recv, tile_sem,
):
    z, x, y, c = place()
    greet(z, x, y, c)

    def columns(h):
        return pl.ds(pl.multiple_of(h * DH, DH), DH)

    def rows(at):
        return pl.ds(pl.multiple_of(at * ROWS, ROWS), ROWS)

    def offsets(a):
        right, left = STEPS[a]
        return range(-left, right + 1)

    def load(a, off):
        at = around(z, off, NZ)
        return pltpu.make_async_copy(part.at[a, at, :, c], own.at[a, at], own_sem.at[a, off + 4])

    def pair(a, off):
        at = around(z, off, NZ)
        return remote(
            part.at[a, at, :, 1 - c], sib.at[a, at], pair_send.at[a, off + 4],
            pair_recv.at[a, off + 4], device(z, x, y, 1 - c),
        )

    for a, off in sorted(((a, off) for a in range(2) for off in offsets(a)), key=lambda m: -abs(m[1])):
        load(a, off).start()
        pair(a, off).start()

    outs = (dk_out, dv_out, att_out, dq_out)

    def source(a, xs, ys):
        if a < 2:
            return own.at[a, z, xs, rows(ys)]
        return (att, dq)[a - 2].at[xs, rows(ys)]

    def tile_out(a, p):
        px, py = (x + p // NY) % NX, (y + p % NY) % NY
        return remote(
            source(a, px, py), outs[a].at[:, columns(x * NY + y)],
            plane_send.at[a, p], plane_recv.at[a, p], device(z, px, py, c),
        )

    def tile_in(a, p):
        px, py = (x + NX - p // NY) % NX, (y + NY - p % NY) % NY
        return remote(
            source(a, x, y), outs[a].at[:, columns(px * NY + py)],
            plane_send.at[a, p], plane_recv.at[a, p], device(z, px, py, c),
        )

    def tile_own(a):
        return pltpu.make_async_copy(source(a, x, y), outs[a].at[:, columns(x * NY + y)], tile_sem.at[a])

    for a in (2, 3):
        tile_own(a).start()

    def start(p, carry):
        tile_out(2, p).start()
        tile_out(3, p).start()
        return carry

    lax.fori_loop(1, NX * NY, start, 0)

    def ring(a, way, step, j):
        sign = 1 if way == 0 else -1
        at = around(z, sign * (STEPS[a][way] - step + 1), NZ)
        return remote(
            own.at[a, at, j], came.at[a, way, step - 1, j], ring_send.at[a, way, step - 1, j],
            ring_recv.at[a, way, step - 1, j], device(around(z, sign, NZ), x, y, c),
        )

    def add(a, off, j, arrived):
        at = around(z, off, NZ)
        total = own[a, at, j].astype(jnp.float32) + sib[a, at, j].astype(jnp.float32)
        for way, step in arrived:
            total += came[a, way, step - 1, j].astype(jnp.float32)
        own[a, at, j] = total.astype(jnp.bfloat16)

    for step in range(1, 5):
        for a in range(2):
            for way in range(2):
                if step <= STEPS[a][way]:
                    off = (1 if way == 0 else -1) * (STEPS[a][way] - step + 1)
                    load(a, off).wait()
                    pair(a, off).wait_recv()

        def chunk_step(j, carry):
            for a in range(2):
                for way in range(2):
                    count = STEPS[a][way]
                    if step <= count:
                        off = (1 if way == 0 else -1) * (count - step + 1)
                        if step > 1:
                            ring(a, way, step - 1, j).wait_recv()
                        add(a, off, j, [(way, step - 1)] if step > 1 else [])
                        ring(a, way, step, j).start()
            return carry

        lax.fori_loop(0, NX, chunk_step, 0)

    for a in range(2):
        load(a, 0).wait()
        pair(a, 0).wait_recv()
    for dx in range(NX):
        j = (x + dx) % NX
        for a in range(2):
            for way in range(2):
                ring(a, way, STEPS[a][way], j).wait_recv()
            add(a, 0, j, [(0, STEPS[a][0]), (1, STEPS[a][1])])
            for dy in range(NY):
                if dx == 0 and dy == 0:
                    tile_own(a).start()
                else:
                    tile_out(a, dx * NY + dy).start()

    def finish_plane(p, carry):
        for a in range(4):
            tile_out(a, p).wait_send()
            tile_in(a, p).wait_recv()
        return carry

    lax.fori_loop(1, NX * NY, finish_plane, 0)
    for a in range(4):
        tile_own(a).wait()

    def finish_ring(j, carry):
        for a in range(2):
            for way in range(2):
                for step in range(1, STEPS[a][way] + 1):
                    ring(a, way, step, j).wait_send()
        return carry

    lax.fori_loop(0, NX, finish_ring, 0)
    for a in range(2):
        for off in offsets(a):
            pair(a, off).wait_send()


ANY = pl.BlockSpec(memory_space=pl.ANY)
VMEM = pl.BlockSpec(memory_space=pltpu.VMEM)
SMEM = pl.BlockSpec(memory_space=pltpu.SMEM)
DMA = pltpu.SemaphoreType.DMA


def bf16(*shape):
    return jax.ShapeDtypeStruct(shape, jnp.bfloat16)


def shards(queries, keys, values, noise, random_blocks, global_blocks):
    z, x, y, c = place()
    q_all, n_all, kv = pl.pallas_call(
        fetch_kernel,
        name="fetch",
        out_shape=(bf16(NX, SHARD, DH), bf16(NX, SHARD, DH), bf16(2, NZ, NX, NC, SHARD, DH)),
        in_specs=[ANY] * 4,
        out_specs=(ANY,) * 3,
        scratch_shapes=[
            DMA((4, NX * NY)), DMA((4, NX * NY)), DMA((4,)),
            DMA((2, 2, 4, NX)), DMA((2, 2, 4, NX)), DMA((2, 9, NX)), DMA((2, 9, NX)),
        ],
        compiler_params=pltpu.CompilerParams(collective_id=0, has_side_effects=True),
    )(queries, keys, values, noise)

    mine = lax.dynamic_index_in_dim(random_blocks.reshape(NZ, NX, NC, PER, 3), z, 0, keepdims=False)
    mine = lax.dynamic_index_in_dim(mine, c, 1, keepdims=False).reshape(QUERIES, 3)
    at = jnp.arange(QUERIES, dtype=jnp.int32)
    firsts = ((z * NX + at // PER) * NC + c) * PER + at % PER
    window = jnp.clip(firsts[:, None] + jnp.arange(-1, 2, dtype=jnp.int32)[None], 0, NB - 1)
    lists = jnp.concatenate(
        [window, mine, jnp.broadcast_to(global_blocks[None], (QUERIES, 2))], 1
    ).astype(jnp.int32)

    att, dq, part = pl.pallas_call(
        attend_kernel,
        name="attend",
        out_shape=(bf16(QUERIES, BLK, DH), bf16(QUERIES, BLK, DH), bf16(2, NB, BLK, DH)),
        in_specs=[SMEM, SMEM, VMEM, VMEM, ANY],
        out_specs=(VMEM, VMEM, ANY),
        scratch_shapes=[
            pltpu.VMEM((2, NB, BLK, DH), jnp.bfloat16),
            pltpu.VMEM((2, NB, BLK, DH), jnp.float32),
            DMA((2,)), DMA((2, NB // 64)),
        ],
        compiler_params=pltpu.CompilerParams(vmem_limit_bytes=60 * 2**20),
    )(
        lists, firsts, q_all.reshape(QUERIES, BLK, DH), n_all.reshape(QUERIES, BLK, DH),
        kv.reshape(2, NB, BLK, DH),
    )

    outs = pl.pallas_call(
        return_kernel,
        name="give_back",
        out_shape=(bf16(ROWS, NX * NY * DH),) * 4,
        in_specs=[ANY] * 3,
        out_specs=(ANY,) * 4,
        scratch_shapes=[
            pltpu.VMEM((2, NZ, NX, SHARD, DH), jnp.bfloat16),
            pltpu.VMEM((2, NZ, NX, SHARD, DH), jnp.bfloat16),
            pltpu.VMEM((2, 2, 4, NX, SHARD, DH), jnp.bfloat16),
            DMA((2, 9)), DMA((2, 9)), DMA((2, 9)),
            DMA((2, 2, 4, NX)), DMA((2, 2, 4, NX)),
            DMA((4, NX * NY)), DMA((4, NX * NY)), DMA((4,)),
        ],
        compiler_params=pltpu.CompilerParams(
            collective_id=1, has_side_effects=True, vmem_limit_bytes=40 * 2**20
        ),
    )(
        att.reshape(NX, SHARD, DH), dq.reshape(NX, SHARD, DH),
        part.reshape(2, NZ, NX, NC, SHARD, DH),
    )
    return tuple(outs)


def solution(mesh):
    rows = P(("seq", "head"), None)
    return jax.shard_map(
        shards,
        mesh=mesh,
        in_specs=(rows, rows, rows, rows, P(), P()),
        out_specs=(rows, rows, rows, rows),
        check_vma=False,
    )
```

time: 737 us -> 248 us (0.34); the launches traced: 727 us -> 248 us
  waiting for transfers between devices: 472 us -> 0 us
  Pallas kernels: 0 us -> 240 us
  starting transfers between devices: 71.1 us -> 0 us
  local copies, waits for them, and re-layouts: 76.7 us -> 7.66 us
  other arithmetic: 67.8 us -> 0.16 us
  matrix products: 19.6 us -> 0 us
  between operations: 20.1 us -> 0.74 us
    psum x2 -> x0, waiting for transfers between devices: 459 us -> none  [the longest x1 231 us: broadcast(): return lax.psum(kept, axis)]
    pallas_call x0 -> x3, Pallas kernels: none -> 240 us  [the longest x1 114 us: shards(): pl.pallas_call(return_kernel, name='give_back', out_shape=(bf16(ROWS, NX...]
    all_to_all x10 -> x0, starting transfers between devices: 64.6 us -> none  [the longest x1 16.8 us: shards(): lax.all_to_all(outgoing, 'seq', split_axis=0, concat_axis=0, tiled=True)]
    scatter-add x4 -> x0, other arithmetic: 23.7 us -> none  [the longest x1 22.8 us: shards(): local_grads.at[send_index]]
    select_n x8 -> x0, other arithmetic: 23.7 us -> none  [the longest x1 12.2 us: shards(): jnp.where(valid_mask, returned.astype(jnp.float32), 0.0)]
    gather x3 -> x0, local copies, waits for them, and re-layouts: 20.9 us -> none  [the longest x2 11.6 us: shards(): jnp.take(incoming, slot_of, axis=0)]
    dot_general x10 -> x0, matrix products: 19.6 us -> none  [the longest x1 5.26 us: shards(): jnp.einsum('ihad,ihkd->ihak', out_grad, value_blocks, preferred_element_t...]
    all_to_all x10 -> x0, waiting for transfers between devices: 10.8 us -> none  [the longest x1 5.22 us: shards(): lax.all_to_all(value_grad, 'head', split_axis=0, concat_axis=1, tiled=True)]
  transfers between devices with their start and end apart: 16 -> 0, of which waited for: 7 -> 0; matrix products, arithmetic and copies ran while one was open for 17% -> 0% of each run, Pallas kernels for 0% -> 0%
where the time goes in v1:
time: 248 us
  Pallas kernels  240 us (97%)
  local copies, waits for them, and re-layouts  7.66 us (3%)
    pallas_call x1, Pallas kernels, shards(): pl.pallas_call(return_kernel, name='give_back', out_shape=(bf16(ROWS, NX...  114 us
    pallas_call x1, Pallas kernels, shards(): pl.pallas_call(fetch_kernel, name='fetch', out_shape=(bf16(NX, SHARD, DH)...  99 us
    pallas_call x1, Pallas kernels, shards(): pl.pallas_call(attend_kernel, name='attend', out_shape=(bf16(QUERIES, BLK...  26.3 us
    unnamed x10, local copies, waits for them, and re-layouts  5.26 us

profile of v1, /device:TPU:8, one launch (start us, length us, event | category | flops | bytes accessed | tf_op | source)
XLA Modules:
  0.0 248.2 jit_solution(1891258257486689622)
XLA Ops:
  0.7 0.0 copy-start.2
  0.7 0.7 pad.2.clone
  1.4 0.1 add_clamp_fusion
  1.5 0.9 reshape.65
  2.4 0.1 reshape.66
  2.5 0.1 add_add_fusion
  2.6 0.7 copy.13.lists
  3.3 99.0 %fetch.1 = (bf16[4,512,128]{2,1,0:T(8,128)(2,1)}, bf16[4,512,128]{2,1,0:T(8,128)(2,1)}, bf16[2,8,4,2,512,128]{5,4,3,2,1,0:T(8,128)(2,1)}) custom-call(bf16[128,2048]{1,0:T(8,128)(2,1)} %q.1, bf16[128,2048]{1,0:T(8,128)(2,1)} %k.1, bf16[128,2048]{1,0:T(8,128)(2,1)} %v.1, bf16[128,2048]{1,0:T(8,128)(2,1)} %n.1), custom_call_target="tpu_custom_call" | custom-call | tf_op jit(solution)/shard_map/fetch/pallas_call | solution.py:428
  102.3 0.0 copy-done.2
  102.3 26.3 %attend.1 = (bf16[32,64,128]{2,1,0:T(8,128)(2,1)}, bf16[32,64,128]{2,1,0:T(8,128)(2,1)}, bf16[2,512,64,128]{3,2,1,0:T(8,128)(2,1)}) custom-call(s32[32,8]{1,0:T(8,128)} %copy.13.lists, s32[32]{0:T(128)} %copy-done.2, bf16[32,64,128]{2,1,0:T(8,128)(2,1)} %bitcast.15, bf16[32,64,128]{2,1,0:T(8,128)(2,1)} %bitcast.16, bf16[2,512,64,128]{3,2,1,0:T(8,128)(2,1)} %bitcast.14), custom_call_target="tpu_custom_call" | custom-call | tf_op jit(solution)/shard_map/attend/pallas_call | solution.py:450
  128.6 0.0 copy-start
  128.6 1.0 copy-done
  129.6 0.0 copy-start.1
  129.6 1.0 copy-done.1
  130.7 114.4 %give_back.1 = (bf16[128,2048]{1,0:T(8,128)(2,1)S(1)}, bf16[128,2048]{1,0:T(8,128)(2,1)S(1)}, bf16[128,2048]{1,0:T(8,128)(2,1)S(1)}, bf16[128,2048]{1,0:T(8,128)(2,1)S(1)}) custom-call(bf16[4,512,128]{2,1,0:T(8,128)(2,1)S(1)} %bitcast.11, bf16[4,512,128]{2,1,0:T(8,128)(2,1)S(1)} %bitcast.12, bf16[2,8,4,2,512,128]{5,4,3,2,1,0:T(8,128)(2,1)} %bitcast.13), custom_call_target="tpu_custom_call" | custom-call | tf_op jit(solution)/shard_map/give_back/pallas_call | solution.py:467
  245.0 0.8 copy.19
  245.8 0.8 copy.20
  246.6 0.8 copy.21
  247.4 0.8 copy.22
  (3 shorter events, 0.0 us)
Async XLA Ops:
  0.7 101.6 %copy-start.2 = (s32[32]{0:T(128)}, s32[32]{0:T(128)S(1)}, u32[]{:S(2)}) copy-start(s32[32]{0:T(128)S(1)} %fusion.firsts) | copy-start | bytes 388
  128.6 1.0 copy-start
  129.6 1.0 copy-start.1

commit v2 on v1

v2 whole, which is shorter than its diff:
```python
import math

import jax
import jax.numpy as jnp
from jax import lax
from jax.experimental import pallas as pl
from jax.experimental.pallas import tpu as pltpu
from jax.sharding import PartitionSpec as P

DH = 128
BLK = 64
NX, NY, NZ, NC = 4, 4, 8, 2
ROWS = 128
SIDE = 2 * ROWS
SHARD = NY * ROWS
PER = SHARD // BLK
NB = NZ * NX * NC * PER
QUERIES = NZ * SIDE // BLK
HEADS = 16
ENTRIES = 8
GROUP = 4
PARTS = NZ // 2
MESH = pl.DeviceIdType.MESH


def place():
    seq, y = lax.axis_index("seq"), lax.axis_index("head")
    return seq // (NX * NC), (seq // NC) % NX, y, seq % NC


def device(z, x, y, c):
    return ((z * NX + x) * NC + c, y)


def around(base, step, count):
    return (base + step + count) % count


def offset(slot):
    return (slot + 1) // 2 * (2 * (slot % 2) - 1)


def beside(y):
    return y + 1 - 2 * (y % 2)


def half(y):
    return (y + 1) // 2 % 2


def greet(z, x, y, c):
    barrier = pltpu.get_barrier_semaphore()

    def signal(target):
        pl.semaphore_signal(barrier, inc=1, device_id=target, device_id_type=MESH)

    def plane(dz, carry):
        signal(device((z + dz) % NZ, x, y, c))
        signal(device((z + dz) % NZ, x, beside(y), c))
        return carry

    lax.fori_loop(1, NZ, plane, 0)
    signal(device(z, x, beside(y), c))
    signal(device(z, around(x, 1, NX), y, c))
    signal(device(z, around(x, -1, NX), y, c))
    signal(device(z, x, NY - 1 - y, c))
    signal(device(z, x, y, 1 - c))
    pl.semaphore_wait(barrier, 2 * NZ - 1 + 4)


def remote(src, dst, send, recv, target):
    return pltpu.make_async_remote_copy(
        src_ref=src, dst_ref=dst, send_sem=send, recv_sem=recv, device_id=target, device_id_type=MESH
    )


def columns(h):
    return pl.ds(pl.multiple_of(h * DH, DH), DH)


def rows(at):
    return pl.ds(pl.multiple_of(at * ROWS, ROWS), ROWS)


def far_way(a, part):
    return 1 if (a + part) % 2 == 0 else -1


LONG1, LONG2, SHORT = 0, 1, 2


def fetch_kernel(
    q, k, v, n, q_out, n_out, kv,
    tile_send, tile_recv, own_sem, x_send, x_recv, y_send, y_recv, pair_send, pair_recv,
):
    z, x, y, c = place()
    greet(z, x, y, c)
    side = y // 2
    sources = (k, v, q, n)

    def landing(a, slot, row):
        if a < 2:
            return kv.at[a, slot, x, c, side, rows(row)]
        return (q_out, n_out)[a - 2].at[slot, rows(row)]

    def tile_out(a, slot, turn):
        tz, ty = (z - offset(slot) + NZ) % NZ, beside(y) if turn else y
        return remote(
            sources[a].at[:, columns(tz * 2 + half(ty))], landing(a, slot, y % 2),
            tile_send.at[a, turn, slot], tile_recv.at[a, turn, slot], device(tz, x, ty, c),
        )

    def tile_in(a, slot, turn):
        fz, fy = (z + offset(slot) + NZ) % NZ, beside(y) if turn else y
        return remote(
            sources[a].at[:, columns(fz * 2 + half(fy))], landing(a, slot, fy % 2),
            tile_send.at[a, turn, slot], tile_recv.at[a, turn, slot], device(fz, x, fy, c),
        )

    def tile_own(a):
        return pltpu.make_async_copy(
            sources[a].at[:, columns(z * 2 + half(y))], landing(a, 0, y % 2), own_sem.at[a]
        )

    for a in range(4):
        tile_own(a).start()
    for first in (0, 2):
        tile_out(first, 0, 1).start()
        tile_out(first + 1, 0, 1).start()

        def start(slot, carry):
            for turn in range(2):
                tile_out(first, slot, turn).start()
                tile_out(first + 1, slot, turn).start()
            return carry

        lax.fori_loop(1, NZ, start, 0)

    def chunk(a, part, dx, core, g):
        return kv.at[a, pl.ds(2 * part, 2), around(x, dx, NX), core, side if g == 0 else 1 - side]

    def along_x(a, part, g, leg):
        way = far_way(a, part)
        dx, to = {LONG1: (0, way), LONG2: (-way, way), SHORT: (0, -way)}[leg]
        ref = chunk(a, part, dx, c, g)
        return remote(
            ref, ref, x_send.at[a, part, g, leg], x_recv.at[a, part, g, leg],
            device(z, around(x, to, NX), y, c),
        )

    def from_x(a, part, g, leg):
        way = far_way(a, part)
        dx, of = {LONG1: (-way, -way), LONG2: (-2 * way, -way), SHORT: (way, way)}[leg]
        ref = chunk(a, part, dx, c, g)
        return dx, remote(
            ref, ref, x_send.at[a, part, g, leg], x_recv.at[a, part, g, leg],
            device(z, around(x, of, NX), y, c),
        )

    def over_y(a, part, dx, g):
        ref = chunk(a, part, dx, c, g)
        return remote(
            ref, ref, y_send.at[a, part, dx % NX], y_recv.at[a, part, dx % NX],
            device(z, x, NY - 1 - y, c),
        )

    def pair(a, part, dx, g, core):
        ref = chunk(a, part, dx, core, g)
        return remote(
            ref, ref, pair_send.at[a, part, g, dx % NX], pair_recv.at[a, part, g, dx % NX],
            device(z, x, y, 1 - c),
        )

    def entered(a, part):
        for slot in (2 * part, 2 * part + 1):
            for turn in range(2):
                if slot == 0 and turn == 0:
                    tile_own(a).wait()
                else:
                    tile_in(a, slot, turn).wait_recv()

    def got_x(a, part, g, leg):
        dx, copy = from_x(a, part, g, leg)
        copy.wait_recv()
        if leg == LONG1:
            along_x(a, part, g, LONG2).start()
        if a == 0:
            over_y(a, part, dx, 0).start()
        pair(a, part, dx, g, c).start()

    def stage_a(part):
        for a in (1, 0):
            entered(a, part)
            if a == 1:
                over_y(a, part, 0, 0).start()
            along_x(a, part, 0, LONG1).start()
            along_x(a, part, 0, SHORT).start()
            if a == 0:
                over_y(a, part, 0, 0).start()
            pair(a, part, 0, 0, c).start()

    def stage_b(part):
        over_y(1, part, 0, 1).wait_recv()
        along_x(1, part, 1, LONG1).start()
        along_x(1, part, 1, SHORT).start()
        pair(1, part, 0, 1, c).start()
        for a in (0, 1):
            got_x(a, part, 0, LONG1)
            got_x(a, part, 0, SHORT)

    def stage_c(part):
        got_x(1, part, 1, LONG1)
        got_x(1, part, 1, SHORT)
        got_x(0, part, 0, LONG2)
        got_x(1, part, 0, LONG2)

    def stage_d(part):
        got_x(1, part, 1, LONG2)
        for dx in range(NX):
            over_y(0, part, dx, 1).wait_recv()
            pair(0, part, dx, 1, c).start()

    stages = (stage_a, stage_b, stage_c, stage_d)
    for time in range(PARTS + len(stages) - 1):
        for late, stage in enumerate(stages):
            if 0 <= time - late < PARTS:
                stage(time - late)

    for a in (2, 3):
        tile_own(a).wait()
    for a in range(4):
        tile_out(a, 0, 1).wait_send()
        if a >= 2:
            tile_in(a, 0, 1).wait_recv()

    def finish(slot, carry):
        for turn in range(2):
            for a in range(4):
                tile_out(a, slot, turn).wait_send()
                if a >= 2:
                    tile_in(a, slot, turn).wait_recv()
        return carry

    lax.fori_loop(1, NZ, finish, 0)
    for part in range(PARTS):
        for a in range(2):
            for g in range(1 + a):
                for leg in range(3):
                    along_x(a, part, g, leg).wait_send()
            for dx in range(NX if a == 0 else 1):
                over_y(a, part, dx, 0).wait_send()
            for g in range(2):
                for dx in range(NX):
                    pair(a, part, dx, g, c).wait_send()
                    pair(a, part, dx, g, 1 - c).wait_recv()


def attend_kernel(
    lists, firsts, q, n, kv_hbm, att, dq, part, kv, acc, load_sem, store_sem,
):
    scaling = 1.0 / math.sqrt(DH)
    loads = [pltpu.make_async_copy(kv_hbm.at[a], kv.at[a], load_sem.at[a]) for a in range(2)]
    for load in loads:
        load.start()

    def clear(i, carry):
        for a in range(2):
            acc[a, pl.ds(i * 8, 8)] = jnp.zeros((8, BLK, DH), jnp.float32)
        return carry

    lax.fori_loop(0, NB // 8, clear, 0)
    for load in loads:
        load.wait()

    column = lax.broadcasted_iota(jnp.int32, (1, ENTRIES * BLK), 1) // BLK

    def dot(a, b, dims):
        return lax.dot_general(a, b, (dims, ((), ())), preferred_element_type=jnp.float32)

    def group(g, carry):
        ids = [g * GROUP + u for u in range(GROUP)]
        entries = [[lists[i, e] for e in range(ENTRIES)] for i in ids]
        qs = [q[i] for i in ids]
        ks = [jnp.concatenate([kv[0, e] for e in es], 0) for es in entries]
        scores = [dot(a, b, ((1,), (1,))) * scaling for a, b in zip(qs, ks)]
        masked = []
        for i, s in zip(ids, scores):
            block = firsts[i]
            gone = ((column == 0) & (block == 0)) | ((column == 2) & (block == NB - 1))
            masked.append(jnp.where(gone, -jnp.inf, s))
        raws = [jnp.exp(s - jnp.max(s, 1, keepdims=True)) for s in masked]
        probs = [r * (1.0 / jnp.sum(r, 1, keepdims=True)) for r in raws]
        probs_bf = [p.astype(jnp.bfloat16) for p in probs]
        vs = [jnp.concatenate([kv[1, e] for e in es], 0) for es in entries]
        atts = [dot(p, b, ((1,), (0,))).astype(jnp.bfloat16) for p, b in zip(probs_bf, vs)]
        grads = []
        for i, a in zip(ids, atts):
            att[i] = a
            grads.append((a.astype(jnp.float32) - n[i].astype(jnp.float32)).astype(jnp.bfloat16))
        dprobs = [dot(d, b, ((1,), (1,))) for d, b in zip(grads, vs)]
        dscores = [
            (p * (d - jnp.sum(p * d, 1, keepdims=True))).astype(jnp.bfloat16)
            for p, d in zip(probs, dprobs)
        ]
        for i, d, b in zip(ids, dscores, ks):
            dq[i] = (dot(d, b, ((1,), (0,))) * scaling).astype(jnp.bfloat16)
        dks = [dot(d, a, ((0,), (0,))) * scaling for d, a in zip(dscores, qs)]
        dvs = [dot(p, d, ((0,), (0,))) for p, d in zip(probs_bf, grads)]
        for es, dk, dv in zip(entries, dks, dvs):
            for e in range(ENTRIES):
                acc[0, es[e]] += dk[e * BLK : (e + 1) * BLK]
                acc[1, es[e]] += dv[e * BLK : (e + 1) * BLK]
        return carry

    lax.fori_loop(0, QUERIES // GROUP, group, 0)

    def store(a, i):
        span = pl.ds(i * 64, 64)
        return pltpu.make_async_copy(kv.at[a, span], part.at[a, span], store_sem.at[a, i])

    for a in range(2):
        def out(i, carry):
            def cast(s, inner):
                at = pl.ds(i * 64 + s * 8, 8)
                kv[a, at] = acc[a, at].astype(jnp.bfloat16)
                return inner

            lax.fori_loop(0, 8, cast, 0)
            store(a, i).start()
            return carry

        lax.fori_loop(0, NB // 64, out, 0)
    for a in range(2):
        def done(i, carry):
            store(a, i).wait()
            return carry

        lax.fori_loop(0, NB // 64, done, 0)


def return_kernel(
    att, dq, part_hbm, att_out, dq_out, dk_out, dv_out,
    own, sib, x_came, y_came, load_sem, pair_send, pair_recv, x_send, x_recv, y_send, y_recv,
    tile_send, tile_recv, tile_sem,
):
    z, x, y, c = place()
    greet(z, x, y, c)
    side = y // 2

    def load(a, part):
        return pltpu.make_async_copy(
            part_hbm.at[a, pl.ds(2 * part, 2), :, c], own.at[a, part], load_sem.at[a, part]
        )

    def pair(a, part):
        return remote(
            part_hbm.at[a, pl.ds(2 * part, 2), :, 1 - c], sib.at[a, part],
            pair_send.at[a, part], pair_recv.at[a, part], device(z, x, y, 1 - c),
        )

    order = tuple(reversed(range(PARTS)))
    for part in order:
        for a in (0, 1):
            pair(a, part).start()
            load(a, part).start()

    outs = (dk_out, dv_out, att_out, dq_out)

    def source(a, slot, row):
        if a < 2:
            return own.at[a, slot // 2, slot % 2, x, side, rows(row)]
        return (att, dq)[a - 2].at[slot, rows(row)]

    def tile_out(a, slot, turn):
        tz, ty = (z + offset(slot) + NZ) % NZ, beside(y) if turn else y
        return remote(
            source(a, slot, ty % 2), outs[a].at[:, columns(z * 2 + half(y))],
            tile_send.at[a, turn, slot], tile_recv.at[a, turn, slot], device(tz, x, ty, c),
        )

    def tile_in(a, slot, turn):
        fz, fy = (z - offset(slot) + NZ) % NZ, beside(y) if turn else y
        return remote(
            source(a, slot, y % 2), outs[a].at[:, columns(fz * 2 + half(fy))],
            tile_send.at[a, turn, slot], tile_recv.at[a, turn, slot], device(fz, x, fy, c),
        )

    def tile_own(a):
        return pltpu.make_async_copy(
            source(a, 0, y % 2), outs[a].at[:, columns(z * 2 + half(y))], tile_sem.at[a]
        )

    for a in (2, 3):
        tile_own(a).start()
        tile_out(a, 0, 1).start()

    def start(slot, carry):
        for turn in range(2):
            tile_out(2, slot, turn).start()
            tile_out(3, slot, turn).start()
        return carry

    lax.fori_loop(1, NZ, start, 0)

    def sum_up(a, part, dx, g, first, came):
        xs, gs = around(x, dx, NX), side if g == 0 else 1 - side

        def span(i, carry):
            at = rows(i % 2)
            total = own[a, part, i // 2, xs, gs, at].astype(jnp.float32)
            if first:
                total += sib[a, part, i // 2, xs, gs, at].astype(jnp.float32)
            for ref in came:
                total += ref[i // 2, at].astype(jnp.float32)
            own[a, part, i // 2, xs, gs, at] = total.astype(jnp.bfloat16)
            return carry

        lax.fori_loop(0, 4, span, 0)

    def chunk(a, part, dx, g):
        return own.at[a, part, :, around(x, dx, NX), side if g == 0 else 1 - side]

    def landed_x(a, part, g, leg):
        return x_came.at[a + g, part, leg]

    def landed_y(a, part, dx):
        return y_came.at[part, dx % NX if a == 0 else NX]

    def along_x(a, part, g, leg):
        way = far_way(a, part)
        dx, to = {LONG1: (2 * way, way), LONG2: (way, way), SHORT: (-way, -way)}[leg]
        return remote(
            chunk(a, part, dx, g), landed_x(a, part, g, leg), x_send.at[a, part, g, leg],
            x_recv.at[a, part, g, leg], device(z, around(x, to, NX), y, c),
        )

    def over_y(a, part, dx):
        return remote(
            chunk(a, part, dx, 1), landed_y(a, part, dx), y_send.at[a, part, dx % NX],
            y_recv.at[a, part, dx % NX], device(z, x, NY - 1 - y, c),
        )

    def send_tiles(a, part):
        for slot in (2 * part, 2 * part + 1):
            for turn in range(2):
                if slot == 0 and turn == 0:
                    tile_own(a).start()
                else:
                    tile_out(a, slot, turn).start()

    def first_legs(a, part, g, first):
        way = far_way(a, part)
        for dx, leg in ((2 * way, LONG1), (-way, SHORT)):
            sum_up(a, part, dx, g, first, [] if a else [landed_y(a, part, dx)])
            along_x(a, part, g, leg).start()

    def second_leg(a, part, g, first):
        along_x(a, part, g, LONG1).wait_recv()
        dx = far_way(a, part)
        came = [landed_x(a, part, g, LONG1)] + ([] if a else [landed_y(a, part, dx)])
        sum_up(a, part, dx, g, first, came)
        along_x(a, part, g, LONG2).start()

    def last_sum(a, part, g, first):
        along_x(a, part, g, LONG2).wait_recv()
        along_x(a, part, g, SHORT).wait_recv()
        came = [landed_x(a, part, g, LONG2), landed_x(a, part, g, SHORT)]
        sum_up(a, part, 0, g, first, came + ([] if a else [landed_y(a, part, 0)]))

    def stage_a(part):
        for a in (0, 1):
            load(a, part).wait()
            pair(a, part).wait_recv()
            if a == 0:
                way = far_way(a, part)
                for dx in (2 * way, -way, way, 0):
                    sum_up(a, part, dx, 1, True, [])
                    over_y(a, part, dx).start()
            else:
                for g in (1, 0):
                    first_legs(a, part, g, True)

    def stage_b(part):
        for dx in range(NX):
            over_y(0, part, dx).wait_recv()
        first_legs(0, part, 0, True)
        second_leg(1, part, 1, True)
        second_leg(1, part, 0, True)

    def stage_c(part):
        second_leg(0, part, 0, True)
        last_sum(1, part, 1, True)
        over_y(1, part, 0).start()

    def stage_d(part):
        last_sum(0, part, 0, True)
        send_tiles(0, part)
        last_sum(1, part, 0, True)
        over_y(1, part, 0).wait_recv()
        sum_up(1, part, 0, 0, False, [landed_y(1, part, 0)])
        send_tiles(1, part)

    stages = (stage_a, stage_b, stage_c, stage_d)
    for time in range(PARTS + len(stages) - 1):
        for late, stage in enumerate(stages):
            if 0 <= time - late < PARTS:
                stage(order[time - late])

    for a in range(4):
        tile_own(a).wait()
        tile_out(a, 0, 1).wait_send()
        tile_in(a, 0, 1).wait_recv()

    def finish(slot, carry):
        for turn in range(2):
            for a in range(4):
                tile_out(a, slot, turn).wait_send()
                tile_in(a, slot, turn).wait_recv()
        return carry

    lax.fori_loop(1, NZ, finish, 0)
    for part in range(PARTS):
        for a in range(2):
            pair(a, part).wait_send()
            for g in range(1 + a):
                for leg in range(3):
                    along_x(a, part, g, leg).wait_send()
            for dx in range(NX if a == 0 else 1):
                over_y(a, part, dx).wait_send()


ANY = pl.BlockSpec(memory_space=pl.ANY)
VMEM = pl.BlockSpec(memory_space=pltpu.VMEM)
SMEM = pl.BlockSpec(memory_space=pltpu.SMEM)
DMA = pltpu.SemaphoreType.DMA


def bf16(*shape):
    return jax.ShapeDtypeStruct(shape, jnp.bfloat16)


def copies(*shape):
    return [DMA(shape), DMA(shape)]


def shards(queries, keys, values, noise, random_blocks, global_blocks):
    z, x, y, c = place()
    gathered = (2, NZ, NX, NC, 2, SIDE, DH)
    q_all, n_all, kv = pl.pallas_call(
        fetch_kernel,
        name="fetch",
        out_shape=(bf16(NZ, SIDE, DH), bf16(NZ, SIDE, DH), bf16(*gathered)),
        in_specs=[ANY] * 4,
        out_specs=(ANY,) * 3,
        scratch_shapes=[
            *copies(4, 2, NZ), DMA((4,)), *copies(2, PARTS, 2, 3), *copies(2, PARTS, NX),
            *copies(2, PARTS, 2, NX),
        ],
        compiler_params=pltpu.CompilerParams(collective_id=0, has_side_effects=True),
    )(queries, keys, values, noise)

    at = jnp.arange(QUERIES, dtype=jnp.int32)
    planes = (z + offset(at // 4) + NZ) % NZ
    firsts = ((planes * NX + x) * NC + c) * PER + y // 2 * 4 + at % 4
    window = jnp.clip(firsts[:, None] + jnp.arange(-1, 2, dtype=jnp.int32)[None], 0, NB - 1)
    lists = jnp.concatenate(
        [window, random_blocks[firsts], jnp.broadcast_to(global_blocks[None], (QUERIES, 2))], 1
    ).astype(jnp.int32)
    away = (lists // 64 - z + NZ) % NZ
    slots = jnp.where(away <= 4, jnp.maximum(2 * away - 1, 0), 2 * (NZ - away))
    lists = slots * 64 + lists % 64

    att, dq, part = pl.pallas_call(
        attend_kernel,
        name="attend",
        out_shape=(bf16(QUERIES, BLK, DH), bf16(QUERIES, BLK, DH), bf16(2, NB, BLK, DH)),
        in_specs=[SMEM, SMEM, VMEM, VMEM, ANY],
        out_specs=(VMEM, VMEM, ANY),
        scratch_shapes=[
            pltpu.VMEM((2, NB, BLK, DH), jnp.bfloat16),
            pltpu.VMEM((2, NB, BLK, DH), jnp.float32),
            DMA((2,)), DMA((2, NB // 64)),
        ],
        compiler_params=pltpu.CompilerParams(vmem_limit_bytes=60 * 2**20),
    )(
        lists, firsts, q_all.reshape(QUERIES, BLK, DH), n_all.reshape(QUERIES, BLK, DH),
        kv.reshape(2, NB, BLK, DH),
    )

    outs = pl.pallas_call(
        return_kernel,
        name="give_back",
        out_shape=(bf16(ROWS, HEADS * DH),) * 4,
        in_specs=[ANY] * 3,
        out_specs=(ANY,) * 4,
        scratch_shapes=[
            pltpu.VMEM((2, PARTS, 2, NX, 2, SIDE, DH), jnp.bfloat16),
            pltpu.VMEM((2, PARTS, 2, NX, 2, SIDE, DH), jnp.bfloat16),
            pltpu.VMEM((3, PARTS, 3, 2, SIDE, DH), jnp.bfloat16),
            pltpu.VMEM((PARTS, NX + 1, 2, SIDE, DH), jnp.bfloat16),
            DMA((2, PARTS)), *copies(2, PARTS), *copies(2, PARTS, 2, 3), *copies(2, PARTS, NX),
            *copies(4, 2, NZ), DMA((4,)),
        ],
        compiler_params=pltpu.CompilerParams(
            collective_id=1, has_side_effects=True, vmem_limit_bytes=40 * 2**20
        ),
    )(att.reshape(NZ, SIDE, DH), dq.reshape(NZ, SIDE, DH), part.reshape(gathered))
    return tuple(outs)


def solution(mesh):
    rows = P(("seq", "head"), None)
    return jax.shard_map(
        shards,
        mesh=mesh,
        in_specs=(rows, rows, rows, rows, P(), P()),
        out_specs=(rows, rows, rows, rows),
        check_vma=False,
    )
```

time: 248 us -> 196 us (0.79)
  Pallas kernels: 240 us -> 187 us
    pallas_call x2, Pallas kernels: 213 us -> 160 us  [the longest x1 83.2 us: shards(): pl.pallas_call(return_kernel, name='give_back', out_shape=(bf16(ROWS, HEA...]
    unnamed x10 -> x11, local copies, waits for them, and re-layouts: 5.26 us -> 6.09 us
where the time goes in v2:
time: 196 us
  Pallas kernels  187 us (95%)
  local copies, waits for them, and re-layouts  7.4 us (4%)
    pallas_call x1, Pallas kernels, shards(): pl.pallas_call(return_kernel, name='give_back', out_shape=(bf16(ROWS, HEA...  83.2 us
    pallas_call x1, Pallas kernels, shards(): pl.pallas_call(fetch_kernel, name='fetch', out_shape=(bf16(NZ, SIDE, DH),...  77.1 us
    pallas_call x1, Pallas kernels, shards(): pl.pallas_call(attend_kernel, name='attend', out_shape=(bf16(QUERIES, BLK...  26.3 us
    unnamed x11, local copies, waits for them, and re-layouts  6.09 us

profile of v2, /device:TPU:8, one launch (start us, length us, event | category | flops | bytes accessed | tf_op | source)
XLA Modules:
  0.0 195.6 jit_solution(9358425047308058594)
XLA Ops:
  0.7 0.0 copy-start.2
  0.8 0.7 pad.2.clone
  1.5 0.1 add_clamp_fusion
  1.6 0.8 copy.19
  2.4 0.6 gather_fusion
  3.0 0.7 fusion.3.lists
  3.7 77.1 %fetch.1 = (bf16[8,256,128]{2,1,0:T(8,128)(2,1)}, bf16[8,256,128]{2,1,0:T(8,128)(2,1)}, bf16[2,8,4,2,2,256,128]{6,5,4,3,2,1,0:T(8,128)(2,1)}) custom-call(bf16[128,2048]{1,0:T(8,128)(2,1)} %q.1, bf16[128,2048]{1,0:T(8,128)(2,1)} %k.1, bf16[128,2048]{1,0:T(8,128)(2,1)} %v.1, bf16[128,2048]{1,0:T(8,128)(2,1)} %n.1), custom_call_target="tpu_custom_call" | custom-call | tf_op jit(solution)/shard_map/fetch/pallas_call | solution.py:549
  80.8 0.0 copy-done.2
  80.9 26.3 %attend.1 = (bf16[32,64,128]{2,1,0:T(8,128)(2,1)}, bf16[32,64,128]{2,1,0:T(8,128)(2,1)}, bf16[2,512,64,128]{3,2,1,0:T(8,128)(2,1)}) custom-call(s32[32,8]{1,0:T(8,128)} %fusion.3.lists, s32[32]{0:T(128)} %copy-done.2, bf16[32,64,128]{2,1,0:T(8,128)(2,1)} %bitcast.12, bf16[32,64,128]{2,1,0:T(8,128)(2,1)} %bitcast.13, bf16[2,512,64,128]{3,2,1,0:T(8,128)(2,1)} %bitcast.11), custom_call_target="tpu_custom_call" | custom-call | tf_op jit(solution)/shard_map/attend/pallas_call | solution.py:573
  107.1 0.0 copy-start
  107.1 1.0 copy-done
  108.2 0.0 copy-start.1
  108.2 1.0 copy-done.1
  109.2 83.2 %give_back.1 = (bf16[128,2048]{1,0:T(8,128)(2,1)S(1)}, bf16[128,2048]{1,0:T(8,128)(2,1)S(1)}, bf16[128,2048]{1,0:T(8,128)(2,1)S(1)}, bf16[128,2048]{1,0:T(8,128)(2,1)S(1)}) custom-call(bf16[8,256,128]{2,1,0:T(8,128)(2,1)S(1)} %bitcast.8, bf16[8,256,128]{2,1,0:T(8,128)(2,1)S(1)} %bitcast.9, bf16[2,8,4,2,2,256,128]{6,5,4,3,2,1,0:T(8,128)(2,1)} %bitcast.10), custom_call_target="tpu_custom_call" | custom-call | tf_op jit(solution)/shard_map/give_back/pallas_call | solution.py:590
  192.5 0.8 copy.33
  193.3 0.8 copy.34
  194.1 0.8 copy.35
  194.8 0.8 copy.36
  (4 shorter events, 0.1 us)
Async XLA Ops:
  0.7 80.1 %copy-start.2 = (s32[32]{0:T(128)}, s32[32]{0:T(128)S(1)}, u32[]{:S(2)}) copy-start(s32[32]{0:T(128)S(1)} %fusion.5.firsts) | copy-start | bytes 388
  107.1 1.0 copy-start
  108.2 1.0 copy-start.1

commit v3 on v2

v3 whole, which is shorter than its diff:
```python
import math

import jax
import jax.numpy as jnp
from jax import lax
from jax.experimental import pallas as pl
from jax.experimental.pallas import tpu as pltpu
from jax.sharding import PartitionSpec as P

DH = 128
BLK = 64
NX, NY, NZ, NC = 4, 4, 8, 2
ROWS = 128
SIDE = 2 * ROWS
SHARD = NY * ROWS
PER = SHARD // BLK
NB = NZ * NX * NC * PER
QUERIES = NZ * SIDE // BLK
HEADS = 16
ENTRIES = 8
GROUP = 8
FETCH_MIB, ATTEND_MIB, RETURN_MIB = 4, 8, 26
MESH = pl.DeviceIdType.MESH


def place():
    seq, y = lax.axis_index("seq"), lax.axis_index("head")
    return seq // (NX * NC), (seq // NC) % NX, y, seq % NC


def device(z, x, y, c):
    return ((z * NX + x) * NC + c, y)


def around(base, step, count):
    return (base + step + count) % count


def offset(slot):
    return (slot + 1) // 2 * (2 * (slot % 2) - 1)


def beside(y):
    return y + 1 - 2 * (y % 2)


def half(y):
    return (y + 1) // 2 % 2


def greet(z, x, y, c):
    barrier = pltpu.get_barrier_semaphore()

    def signal(target):
        pl.semaphore_signal(barrier, inc=1, device_id=target, device_id_type=MESH)

    def plane(dz, carry):
        signal(device((z + dz) % NZ, x, y, c))
        signal(device((z + dz) % NZ, x, beside(y), c))
        return carry

    lax.fori_loop(1, NZ, plane, 0)
    signal(device(z, x, beside(y), c))
    signal(device(z, around(x, 1, NX), y, c))
    signal(device(z, around(x, -1, NX), y, c))
    signal(device(z, x, NY - 1 - y, c))
    signal(device(z, x, y, 1 - c))
    pl.semaphore_wait(barrier, 2 * NZ - 1 + 4)


def remote(src, dst, send, recv, target):
    return pltpu.make_async_remote_copy(
        src_ref=src, dst_ref=dst, send_sem=send, recv_sem=recv, device_id=target, device_id_type=MESH
    )


def columns(h):
    return pl.ds(pl.multiple_of(h * DH, DH), DH)


def rows(at):
    return pl.ds(pl.multiple_of(at * ROWS, ROWS), ROWS)


def far_way(a, part):
    return 1 if (a + part) % 2 == 0 else -1


def x_first(a, part):
    return a == 0 and part != 4


def sides(a, part):
    return (0,) if x_first(a, part) else (1, 0)


def over_count(a, part):
    return NX if x_first(a, part) else 1


LONG1, LONG2, SHORT = 0, 1, 2


def fetch_kernel(
    q, k, v, n, q_out, n_out, kv, cleared,
    tile_send, tile_recv, own_sem, x_send, x_recv, y_send, y_recv, pair_send, pair_recv,
    zeros, clear_sem,
):
    z, x, y, c = place()
    greet(z, x, y, c)
    side = y // 2
    sources = (k, v, q, n)

    def landing(a, slot, row):
        if a < 2:
            return kv.at[a, slot, x, c, side, rows(row)]
        return (q_out, n_out)[a - 2].at[slot, rows(row)]

    def tile_out(a, slot, turn):
        tz, ty = (z - offset(slot) + NZ) % NZ, beside(y) if turn else y
        return remote(
            sources[a].at[:, columns(tz * 2 + half(ty))], landing(a, slot, y % 2),
            tile_send.at[a, turn, slot], tile_recv.at[a, turn, slot], device(tz, x, ty, c),
        )

    def tile_in(a, slot, turn):
        fz, fy = (z + offset(slot) + NZ) % NZ, beside(y) if turn else y
        return remote(
            sources[a].at[:, columns(fz * 2 + half(fy))], landing(a, slot, fy % 2),
            tile_send.at[a, turn, slot], tile_recv.at[a, turn, slot], device(fz, x, fy, c),
        )

    def tile_own(a):
        return pltpu.make_async_copy(
            sources[a].at[:, columns(z * 2 + half(y))], landing(a, 0, y % 2), own_sem.at[a]
        )

    for a in range(4):
        tile_own(a).start()

    def send_tiles(first):
        tile_out(first, 0, 1).start()
        tile_out(first + 1, 0, 1).start()

        def start(slot, carry):
            for turn in range(2):
                tile_out(first, slot, turn).start()
                tile_out(first + 1, slot, turn).start()
            return carry

        lax.fori_loop(1, NZ, start, 0)

    send_tiles(0)

    def chunk(a, part, dx, core, g):
        return kv.at[a, part, around(x, dx, NX), core, side if g == 0 else 1 - side]

    def along_x(a, part, g, leg):
        way = far_way(a, part)
        dx, to = {LONG1: (0, way), LONG2: (-way, way), SHORT: (0, -way)}[leg]
        ref = chunk(a, part, dx, c, g)
        return remote(
            ref, ref, x_send.at[a, part, g, leg], x_recv.at[a, part, g, leg],
            device(z, around(x, to, NX), y, c),
        )

    def from_x(a, part, g, leg):
        way = far_way(a, part)
        dx, of = {LONG1: (-way, -way), LONG2: (-2 * way, -way), SHORT: (way, way)}[leg]
        ref = chunk(a, part, dx, c, g)
        return dx, remote(
            ref, ref, x_send.at[a, part, g, leg], x_recv.at[a, part, g, leg],
            device(z, around(x, of, NX), y, c),
        )

    def over_y(a, part, dx, g):
        ref = chunk(a, part, dx, c, g)
        return remote(
            ref, ref, y_send.at[a, part, dx % NX], y_recv.at[a, part, dx % NX],
            device(z, x, NY - 1 - y, c),
        )

    def pair(a, part, dx, g, core):
        ref = chunk(a, part, dx, core, g)
        return remote(
            ref, ref, pair_send.at[a, part, g, dx % NX], pair_recv.at[a, part, g, dx % NX],
            device(z, x, y, 1 - c),
        )

    def entered(a, part):
        for turn in range(2):
            if part == 0 and turn == 0:
                tile_own(a).wait()
            else:
                tile_in(a, part, turn).wait_recv()

    def got_x(a, part, g, leg):
        dx, copy = from_x(a, part, g, leg)
        copy.wait_recv()
        if leg == LONG1:
            along_x(a, part, g, LONG2).start()
        if x_first(a, part):
            over_y(a, part, dx, 0).start()
        pair(a, part, dx, g, c).start()

    def stage_a(part):
        for a in (1, 0):
            entered(a, part)
            over_y(a, part, 0, 0).start()
            along_x(a, part, 0, LONG1).start()
            along_x(a, part, 0, SHORT).start()
            pair(a, part, 0, 0, c).start()

    def stage_b(part):
        for a in (1, 0):
            if not x_first(a, part):
                over_y(a, part, 0, 1).wait_recv()
                along_x(a, part, 1, LONG1).start()
                along_x(a, part, 1, SHORT).start()
                pair(a, part, 0, 1, c).start()
        for a in (0, 1):
            got_x(a, part, 0, LONG1)
            got_x(a, part, 0, SHORT)

    def stage_c(part):
        for a in (1, 0):
            if not x_first(a, part):
                got_x(a, part, 1, LONG1)
                got_x(a, part, 1, SHORT)
        got_x(0, part, 0, LONG2)
        got_x(1, part, 0, LONG2)

    def stage_d(part):
        for a in (1, 0):
            if x_first(a, part):
                for dx in range(NX):
                    over_y(a, part, dx, 1).wait_recv()
                    pair(a, part, dx, 1, c).start()
            else:
                got_x(a, part, 1, LONG2)

    def clear(a, i):
        return pltpu.make_async_copy(zeros, cleared.at[a, pl.ds(i * 64, 64)], clear_sem.at[a, i])

    stages = (stage_a, stage_b, stage_c, stage_d)
    for time in range(NZ + len(stages) - 1):
        for late, stage in enumerate(stages):
            if 0 <= time - late < NZ:
                stage(time - late)
        if time == 0:
            zeros[...] = jnp.zeros(zeros.shape, jnp.bfloat16)
            for a in range(2):
                for i in range(NB // 64):
                    clear(a, i).start()
        if time == 4:
            send_tiles(2)

    for a in range(2):
        for i in range(NB // 64):
            clear(a, i).wait()
    for a in (2, 3):
        tile_own(a).wait()
    for a in range(4):
        tile_out(a, 0, 1).wait_send()
        if a >= 2:
            tile_in(a, 0, 1).wait_recv()

    def finish(slot, carry):
        for turn in range(2):
            for a in range(4):
                tile_out(a, slot, turn).wait_send()
                if a >= 2:
                    tile_in(a, slot, turn).wait_recv()
        return carry

    lax.fori_loop(1, NZ, finish, 0)
    for part in range(NZ):
        for a in range(2):
            for g in sides(a, part):
                for leg in range(3):
                    along_x(a, part, g, leg).wait_send()
            for dx in range(over_count(a, part)):
                over_y(a, part, dx, 0).wait_send()
            for g in range(2):
                for dx in range(NX):
                    pair(a, part, dx, g, c).wait_send()
                    pair(a, part, dx, g, 1 - c).wait_recv()


def attend_kernel(random_blocks, global_blocks, q, n, kv, cleared, att, dq, acc, global_sum):
    scaling = 1.0 / math.sqrt(DH)
    z, x, y, c = place()
    side = y // 2
    global_sum[...] = jnp.zeros(global_sum.shape, jnp.float32)
    column = lax.broadcasted_iota(jnp.int32, (1, ENTRIES * BLK), 1) // BLK

    def lies(block):
        away = ((block >> 6) - z) & (NZ - 1)
        slot = jnp.where(away <= NZ // 2, jnp.maximum(2 * away - 1, 0), 2 * (NZ - away))
        return slot * 64 + (block & 63)

    def dot(a, b, dims):
        return lax.dot_general(a, b, (dims, ((), ())), preferred_element_type=jnp.float32)

    globals_at = [lies(global_blocks[e]) for e in range(2)]

    def add(a, at, term):
        acc[a, at] = (acc[a, at].astype(jnp.float32) + term).astype(jnp.bfloat16)

    def group(g, carry):
        ids = [g * GROUP + u for u in range(GROUP)]
        blocks, entries = [], []
        for u in range(GROUP):
            plane = (z + offset(g * (GROUP // 4) + u // 4)) & (NZ - 1)
            block = ((plane * NX + x) * NC + c) * PER + side * 4 + u % 4
            blocks.append(block)
            near = [jnp.maximum(block - 1, 0), block, jnp.minimum(block + 1, NB - 1)]
            near += [random_blocks[e, block] for e in range(3)]
            entries.append([lies(b) for b in near] + globals_at)
        qs = [q[i] for i in ids]
        ks = [jnp.concatenate([kv[0, e] for e in es], 0) for es in entries]
        scores = [dot(a, b, ((1,), (1,))) * scaling for a, b in zip(qs, ks)]
        masked = []
        for u, (block, s) in enumerate(zip(blocks, scores)):
            if u % 4 == 0:
                s = jnp.where((column == 0) & (block == 0), -jnp.inf, s)
            if u % 4 == 3:
                s = jnp.where((column == 2) & (block == NB - 1), -jnp.inf, s)
            masked.append(s)
        raws = [jnp.exp(s - jnp.max(s, 1, keepdims=True)) for s in masked]
        probs = [r * (1.0 / jnp.sum(r, 1, keepdims=True)) for r in raws]
        probs_bf = [p.astype(jnp.bfloat16) for p in probs]
        vs = [jnp.concatenate([kv[1, e] for e in es], 0) for es in entries]
        atts = [dot(p, b, ((1,), (0,))).astype(jnp.bfloat16) for p, b in zip(probs_bf, vs)]
        grads = []
        for i, a in zip(ids, atts):
            att[i] = a
            grads.append((a.astype(jnp.float32) - n[i].astype(jnp.float32)).astype(jnp.bfloat16))
        dprobs = [dot(d, b, ((1,), (1,))) for d, b in zip(grads, vs)]
        dscores = [
            (p * (d - jnp.sum(p * d, 1, keepdims=True))).astype(jnp.bfloat16)
            for p, d in zip(probs, dprobs)
        ]
        for i, d, b in zip(ids, dscores, ks):
            dq[i] = (dot(d, b, ((1,), (0,))) * scaling).astype(jnp.bfloat16)
        terms = (
            [dot(d, a, ((0,), (0,))) * scaling for d, a in zip(dscores, qs)],
            [dot(p, d, ((0,), (0,))) for p, d in zip(probs_bf, grads)],
        )

        for a in range(2):
            def term(u, e):
                return terms[a][u][e * BLK : (e + 1) * BLK]

            for first in range(0, GROUP, 4):
                last = first + 3
                add(a, entries[first][0], term(first, 0))
                for u in range(first, last + 1):
                    total = term(u, 1)
                    if u > first:
                        total += term(u - 1, 2)
                    if u < last:
                        total += term(u + 1, 0)
                    add(a, entries[u][1], total)
                add(a, entries[last][2], term(last, 2))
            for u in range(GROUP):
                for e in range(3, 6):
                    add(a, entries[u][e], term(u, e))
            for e in range(2):
                global_sum[a, e] += sum(term(u, 6 + e) for u in range(GROUP))
        return carry

    lax.fori_loop(0, QUERIES // GROUP, group, 0)
    for a in range(2):
        for e in range(2):
            add(a, globals_at[e], global_sum[a, e])


def return_kernel(
    att, dq, partial, att_out, dq_out, dk_out, dv_out,
    own, sib, x_came, y_came, pair_send, pair_recv, x_send, x_recv, y_send, y_recv,
    tile_send, tile_recv, tile_sem,
):
    z, x, y, c = place()
    greet(z, x, y, c)
    side = y // 2

    def pair(a, part):
        return remote(
            partial.at[a, part, :, 1 - c], sib.at[a, part],
            pair_send.at[a, part], pair_recv.at[a, part], device(z, x, y, 1 - c),
        )

    order = tuple(reversed(range(NZ)))
    for part in order:
        for a in (0, 1):
            pair(a, part).start()

    outs = (dk_out, dv_out, att_out, dq_out)

    def source(a, slot, row):
        if a < 2:
            return own.at[a, slot, x, side, rows(row)]
        return (att, dq)[a - 2].at[slot, rows(row)]

    def tile_out(a, slot, turn):
        tz, ty = (z + offset(slot) + NZ) % NZ, beside(y) if turn else y
        return remote(
            source(a, slot, ty % 2), outs[a].at[:, columns(z * 2 + half(y))],
            tile_send.at[a, turn, slot], tile_recv.at[a, turn, slot], device(tz, x, ty, c),
        )

    def tile_in(a, slot, turn):
        fz, fy = (z - offset(slot) + NZ) % NZ, beside(y) if turn else y
        return remote(
            source(a, slot, y % 2), outs[a].at[:, columns(fz * 2 + half(fy))],
            tile_send.at[a, turn, slot], tile_recv.at[a, turn, slot], device(fz, x, fy, c),
        )

    def tile_own(a):
        return pltpu.make_async_copy(
            source(a, 0, y % 2), outs[a].at[:, columns(z * 2 + half(y))], tile_sem.at[a]
        )

    for a in (2, 3):
        tile_own(a).start()
        tile_out(a, 0, 1).start()

    def start(slot, carry):
        for turn in range(2):
            tile_out(2, slot, turn).start()
            tile_out(3, slot, turn).start()
        return carry

    lax.fori_loop(1, NZ, start, 0)

    def sum_up(a, part, dx, g, first, came):
        xs, gs = around(x, dx, NX), side if g == 0 else 1 - side

        def span(i, carry):
            at = rows(i)
            if first:
                total = partial[a, part, xs, c, gs, at].astype(jnp.float32)
                total += sib[a, part, xs, gs, at].astype(jnp.float32)
            else:
                total = own[a, part, xs, gs, at].astype(jnp.float32)
            for ref in came:
                total += ref[at].astype(jnp.float32)
            own[a, part, xs, gs, at] = total.astype(jnp.bfloat16)
            return carry

        lax.fori_loop(0, 2, span, 0)

    def chunk(a, part, dx, g):
        return own.at[a, part, around(x, dx, NX), side if g == 0 else 1 - side]

    def landed_x(a, part, g, leg):
        return x_came.at[2 * a + g, part, leg]

    def landed_y(a, part, dx):
        return y_came.at[part, dx % NX if a == 0 else NX]

    def along_x(a, part, g, leg):
        way = far_way(a, part)
        dx, to = {LONG1: (2 * way, way), LONG2: (way, way), SHORT: (-way, -way)}[leg]
        return remote(
            chunk(a, part, dx, g), landed_x(a, part, g, leg), x_send.at[a, part, g, leg],
            x_recv.at[a, part, g, leg], device(z, around(x, to, NX), y, c),
        )

    def over_y(a, part, dx):
        return remote(
            chunk(a, part, dx, 1), landed_y(a, part, dx), y_send.at[a, part, dx % NX],
            y_recv.at[a, part, dx % NX], device(z, x, NY - 1 - y, c),
        )

    def send_tiles(a, part):
        for turn in range(2):
            if part == 0 and turn == 0:
                tile_own(a).start()
            else:
                tile_out(a, part, turn).start()

    def leg(a, part, g, dx, name, came):
        if x_first(a, part):
            over_y(a, part, dx).wait_recv()
            came = came + [landed_y(a, part, dx)]
        sum_up(a, part, dx, g, True, came)
        along_x(a, part, g, name).start()

    def first_legs(a, part):
        way = far_way(a, part)
        for g in sides(a, part):
            leg(a, part, g, 2 * way, LONG1, [])
            leg(a, part, g, -way, SHORT, [])

    def last_sum(a, part, g):
        along_x(a, part, g, LONG2).wait_recv()
        along_x(a, part, g, SHORT).wait_recv()
        came = [landed_x(a, part, g, LONG2), landed_x(a, part, g, SHORT)]
        if x_first(a, part):
            over_y(a, part, 0).wait_recv()
            came = came + [landed_y(a, part, 0)]
        sum_up(a, part, 0, g, True, came)

    def begin(part):
        for a in range(2):
            pair(a, part).wait_recv()
            if x_first(a, part):
                way = far_way(a, part)
                for dx in (2 * way, -way, way, 0):
                    sum_up(a, part, dx, 1, True, [])
                    over_y(a, part, dx).start()
            else:
                first_legs(a, part)

    def after_y(part):
        for a in range(2):
            if x_first(a, part):
                first_legs(a, part)

    def seconds(part):
        for a in (1, 0):
            for g in sides(a, part):
                along_x(a, part, g, LONG1).wait_recv()
                leg(a, part, g, far_way(a, part), LONG2, [landed_x(a, part, g, LONG1)])

    def over(part):
        for a in (1, 0):
            if not x_first(a, part):
                last_sum(a, part, 1)
                over_y(a, part, 0).start()

    def lasts(part):
        for a in range(2):
            last_sum(a, part, 0)
            if not x_first(a, part):
                over_y(a, part, 0).wait_recv()
                sum_up(a, part, 0, 0, False, [landed_y(a, part, 0)])
            send_tiles(a, part)

    plan = ((after_y, 1), (begin, 0), (seconds, 2), (over, 3), (lasts, 4))
    for time in range(NZ + 4):
        for stage, late in plan:
            if 0 <= time - late < NZ:
                stage(order[time - late])

    for a in range(4):
        tile_own(a).wait()
        tile_out(a, 0, 1).wait_send()
        tile_in(a, 0, 1).wait_recv()

    def finish(slot, carry):
        for turn in range(2):
            for a in range(4):
                tile_out(a, slot, turn).wait_send()
                tile_in(a, slot, turn).wait_recv()
        return carry

    lax.fori_loop(1, NZ, finish, 0)
    for part in range(NZ):
        for a in range(2):
            pair(a, part).wait_send()
            for g in sides(a, part):
                for name in range(3):
                    along_x(a, part, g, name).wait_send()
            for dx in range(over_count(a, part)):
                over_y(a, part, dx).wait_send()


def write_kernel(*refs):
    moves = [pltpu.make_async_copy(refs[i], refs[4 + i], refs[8].at[i]) for i in range(4)]
    for move in moves:
        move.start()
    for move in moves:
        move.wait()


ANY = pl.BlockSpec(memory_space=pl.ANY)
VMEM = pl.BlockSpec(memory_space=pltpu.VMEM)
SMEM = pl.BlockSpec(memory_space=pltpu.SMEM)
DMA = pltpu.SemaphoreType.DMA


def bf16(*shape):
    return jax.ShapeDtypeStruct(shape, jnp.bfloat16)


def copies(*shape):
    return [DMA(shape), DMA(shape)]


def shards(queries, keys, values, noise, random_blocks, global_blocks):
    gathered = (2, NZ, NX, NC, 2, SIDE, DH)
    q_all, n_all, kv, cleared = pl.pallas_call(
        fetch_kernel,
        name="fetch",
        out_shape=(
            bf16(NZ, SIDE, DH), bf16(NZ, SIDE, DH), bf16(*gathered), bf16(2, NB, BLK, DH)
        ),
        in_specs=[ANY] * 4,
        out_specs=(ANY, ANY, ANY, ANY),
        scratch_shapes=[
            *copies(4, 2, NZ), DMA((4,)), *copies(2, NZ, 2, 3), *copies(2, NZ, NX),
            *copies(2, NZ, 2, NX), pltpu.VMEM((64, BLK, DH), jnp.bfloat16), DMA((2, NB // 64)),
        ],
        compiler_params=pltpu.CompilerParams(
            collective_id=0, has_side_effects=True, vmem_limit_bytes=FETCH_MIB * 2**20
        ),
    )(queries, keys, values, noise)

    att, dq, partial = pl.pallas_call(
        attend_kernel,
        name="attend",
        out_shape=(bf16(QUERIES, BLK, DH), bf16(QUERIES, BLK, DH), bf16(2, NB, BLK, DH)),
        in_specs=[SMEM, SMEM, VMEM, VMEM, VMEM, VMEM],
        out_specs=(VMEM, VMEM, VMEM),
        scratch_shapes=[pltpu.VMEM((2, 2, BLK, DH), jnp.float32)],
        input_output_aliases={5: 2},
        compiler_params=pltpu.CompilerParams(vmem_limit_bytes=ATTEND_MIB * 2**20),
    )(
        random_blocks.T, global_blocks, q_all.reshape(QUERIES, BLK, DH),
        n_all.reshape(QUERIES, BLK, DH), kv.reshape(2, NB, BLK, DH), cleared,
    )

    outs = pl.pallas_call(
        return_kernel,
        name="give_back",
        out_shape=(bf16(ROWS, HEADS * DH),) * 4,
        in_specs=[ANY, ANY, VMEM],
        out_specs=(ANY,) * 4,
        scratch_shapes=[
            pltpu.VMEM((2, NZ, NX, 2, SIDE, DH), jnp.bfloat16),
            pltpu.VMEM((2, NZ, NX, 2, SIDE, DH), jnp.bfloat16),
            pltpu.VMEM((4, NZ, 3, SIDE, DH), jnp.bfloat16),
            pltpu.VMEM((NZ, NX + 1, SIDE, DH), jnp.bfloat16),
            *copies(2, NZ), *copies(2, NZ, 2, 3), *copies(2, NZ, NX),
            *copies(4, 2, NZ), DMA((4,)),
        ],
        compiler_params=pltpu.CompilerParams(
            collective_id=1, has_side_effects=True, vmem_limit_bytes=RETURN_MIB * 2**20
        ),
    )(att.reshape(NZ, SIDE, DH), dq.reshape(NZ, SIDE, DH), partial.reshape(gathered))
    return pl.pallas_call(
        write_kernel,
        name="write",
        out_shape=(bf16(ROWS, HEADS * DH),) * 4,
        in_specs=[VMEM] * 4,
        out_specs=(ANY,) * 4,
        scratch_shapes=[DMA((4,))],
        compiler_params=pltpu.CompilerParams(vmem_limit_bytes=2**20),
    )(*outs)


def solution(mesh):
    rows = P(("seq", "head"), None)
    return jax.shard_map(
        shards,
        mesh=mesh,
        in_specs=(rows, rows, rows, rows, P(), P()),
        out_specs=(rows, rows, rows, rows),
        check_vma=False,
    )
```

time: 196 us -> 170 us (0.87)
  Pallas kernels: 187 us -> 164 us
    pallas_call x1, Pallas kernels: 26.3 us -> 10.5 us  [shards(): pl.pallas_call(attend_kernel, name='attend', out_shape=(bf16(QUERIES, BLK...]
    pallas_call x1, Pallas kernels: 83.2 us -> 75.3 us  [shards(): pl.pallas_call(return_kernel, name='give_back', out_shape=(bf16(ROWS, HEA...]
    unnamed x11 -> x12, local copies, waits for them, and re-layouts: 6.09 us -> 5.5 us
where the time goes in v3:
time: 170 us
  Pallas kernels  164 us (96%)
  local copies, waits for them, and re-layouts  5.5 us (3%)
    pallas_call x1, Pallas kernels, shards(): pl.pallas_call(fetch_kernel, name='fetch', out_shape=(bf16(NZ, SIDE, DH),...  76.9 us
    pallas_call x1, Pallas kernels, shards(): pl.pallas_call(return_kernel, name='give_back', out_shape=(bf16(ROWS, HEA...  75.3 us
    pallas_call x1, Pallas kernels, shards(): pl.pallas_call(attend_kernel, name='attend', out_shape=(bf16(QUERIES, BLK...  10.5 us
    unnamed x12, local copies, waits for them, and re-layouts  5.5 us

profile of v3, /device:TPU:8, one launch (start us, length us, event | category | flops | bytes accessed | tf_op | source)
XLA Modules:
  0.0 170.2 jit_solution(17928963924879146086)
XLA Ops:
  0.6 0.0 copy-start
  0.6 1.0 copy-done
  1.7 0.0 copy-start.1
  1.7 1.0 copy-done.1
  2.7 0.0 copy-start.2
  2.7 1.0 copy-done.2
  3.8 0.0 copy-start.3
  3.8 1.0 copy-done.3
  4.8 76.9 %fetch.1 = (bf16[8,256,128]{2,1,0:T(8,128)(2,1)S(1)}, bf16[8,256,128]{2,1,0:T(8,128)(2,1)S(1)}, bf16[2,8,4,2,2,256,128]{6,5,4,3,2,1,0:T(8,128)(2,1)S(1)}, bf16[2,512,64,128]{3,2,1,0:T(8,128)(2,1)S(1)}) custom-call(bf16[128,2048]{1,0:T(8,128)(2,1)S(1)} %copy-done, bf16[128,2048]{1,0:T(8,128)(2,1)S(1)} %copy-done.1, bf16[128,2048]{1,0:T(8,128)(2,1)S(1)} %copy-done.2, ...), custom_call_target="tpu_custom_call" | custom-call | tf_op jit(solution)/shard_map/fetch/pallas_call | solution.py:595
  81.7 0.0 copy-start.4
  81.7 0.7 copy-done.4
  82.4 0.0 copy-start.5
  82.4 0.7 copy-done.5
  83.0 10.5 %attend.1 = (bf16[32,64,128]{2,1,0:T(8,128)(2,1)S(1)}, bf16[32,64,128]{2,1,0:T(8,128)(2,1)S(1)}, bf16[2,512,64,128]{3,2,1,0:T(8,128)(2,1)S(1)}) custom-call(s32[3,512]{1,0:T(4,128)S(1)} %bitcast.13, s32[2]{0:T(128)S(1)} %copy-done.5, bf16[32,64,128]{2,1,0:T(8,128)(2,1)S(1)} %bitcast.11, ...), custom_call_target="tpu_custom_call", output_to_operand_aliasing={{2}: (5, {})} | custom-call | tf_op jit(solution)/shard_map/attend/pallas_call | solution.py:612
  93.5 75.3 %give_back.1 = (bf16[128,2048]{1,0:T(8,128)(2,1)S(1)}, bf16[128,2048]{1,0:T(8,128)(2,1)S(1)}, bf16[128,2048]{1,0:T(8,128)(2,1)S(1)}, bf16[128,2048]{1,0:T(8,128)(2,1)S(1)}) custom-call(bf16[8,256,128]{2,1,0:T(8,128)(2,1)S(1)} %bitcast.9, bf16[8,256,128]{2,1,0:T(8,128)(2,1)S(1)} %bitcast.10, bf16[2,8,4,2,2,256,128]{6,5,4,3,2,1,0:T(8,128)(2,1)S(1)} %bitcast.7), custom_call_target="tpu_custom_call" | custom-call | tf_op jit(solution)/shard_map/give_back/pallas_call | solution.py:626
  168.8 1.3 write.1
Async XLA Ops:
  0.6 1.0 copy-start
  1.7 1.0 copy-start.1
  2.7 1.0 copy-start.2
  3.8 1.0 copy-start.3
  81.7 0.7 copy-start.4
  82.4 0.7 copy-start.5

commit v4 on v3

--- a/solution.py
+++ b/solution.py
@@ -25,7 +25,7 @@
 
 def place():
     seq, y = lax.axis_index("seq"), lax.axis_index("head")
-    return seq // (NX * NC), (seq // NC) % NX, y, seq % NC
+    return lax.div(seq, NX * NC), lax.rem(lax.div(seq, NC), NX), y, lax.rem(seq, NC)
 
 
 def device(z, x, y, c):
@@ -33,7 +33,7 @@
 
 
 def around(base, step, count):
-    return (base + step + count) % count
+    return lax.rem(base + step % count, count)
 
 
 def offset(slot):
@@ -41,11 +41,11 @@
 
 
 def beside(y):
-    return y + 1 - 2 * (y % 2)
+    return y + 1 - 2 * lax.rem(y, 2)
 
 
 def half(y):
-    return (y + 1) // 2 % 2
+    return lax.rem(lax.div(y + 1, 2), 2)
 
 
 def greet(z, x, y, c):
@@ -54,12 +54,9 @@
     def signal(target):
         pl.semaphore_signal(barrier, inc=1, device_id=target, device_id_type=MESH)
 
-    def plane(dz, carry):
-        signal(device((z + dz) % NZ, x, y, c))
-        signal(device((z + dz) % NZ, x, beside(y), c))
-        return carry
-
-    lax.fori_loop(1, NZ, plane, 0)
+    for dz in range(1, NZ):
+        signal(device(around(z, dz, NZ), x, y, c))
+        signal(device(around(z, dz, NZ), x, beside(y), c))
     signal(device(z, x, beside(y), c))
     signal(device(z, around(x, 1, NX), y, c))
     signal(device(z, around(x, -1, NX), y, c))
@@ -98,126 +95,118 @@
     return NX if x_first(a, part) else 1
 
 
+def part_count(a, g):
+    return sum(g in sides(a, part) for part in range(NZ))
+
+
 LONG1, LONG2, SHORT = 0, 1, 2
 
 
 def fetch_kernel(
-    q, k, v, n, q_out, n_out, kv, cleared,
+    sources, q_out, n_out, kv, cleared,
     tile_send, tile_recv, own_sem, x_send, x_recv, y_send, y_recv, pair_send, pair_recv,
     zeros, clear_sem,
 ):
     z, x, y, c = place()
     greet(z, x, y, c)
-    side = y // 2
-    sources = (k, v, q, n)
-
-    def landing(a, slot, row):
+    side, odd = lax.div(y, 2), lax.rem(y, 2)
+    xs = [around(x, dx, NX) for dx in range(NX)]
+    other_y = beside(y)
+    mine, theirs = half(y), half(other_y)
+    to_x = {1: device(z, xs[1], y, c), -1: device(z, xs[-1], y, c)}
+    to_y, to_core = device(z, x, NY - 1 - y, c), device(z, x, y, 1 - c)
+
+    def tile_out(a, slot, turn):
+        tz = around(z, -offset(slot), NZ)
         if a < 2:
-            return kv.at[a, slot, x, c, side, rows(row)]
-        return (q_out, n_out)[a - 2].at[slot, rows(row)]
-
-    def tile_out(a, slot, turn):
-        tz, ty = (z - offset(slot) + NZ) % NZ, beside(y) if turn else y
+            dst = kv.at[a, slot, x, c, side, rows(odd)]
+        else:
+            dst = (q_out, n_out)[a - 2].at[slot, rows(odd)]
         return remote(
-            sources[a].at[:, columns(tz * 2 + half(ty))], landing(a, slot, y % 2),
-            tile_send.at[a, turn, slot], tile_recv.at[a, turn, slot], device(tz, x, ty, c),
+            sources.at[a, :, columns(tz * 2 + (theirs if turn else mine))], dst, tile_send.at[a, turn],
+            tile_recv.at[a, slot if a < 2 else turn], device(tz, x, other_y if turn else y, c),
         )
 
-    def tile_in(a, slot, turn):
-        fz, fy = (z + offset(slot) + NZ) % NZ, beside(y) if turn else y
-        return remote(
-            sources[a].at[:, columns(fz * 2 + half(fy))], landing(a, slot, fy % 2),
-            tile_send.at[a, turn, slot], tile_recv.at[a, turn, slot], device(fz, x, fy, c),
-        )
+    def tiles(a, turn):
+        slots = pl.ds(0, NZ - 1 + turn)
+        if a < 2:
+            ref = kv.at[a, slots, x, c, side, rows(0)]
+        else:
+            ref = (q_out, n_out)[a - 2].at[slots, rows(0)]
+        return remote(ref, ref, tile_send.at[a, turn], tile_recv.at[a, turn], to_y)
 
     def tile_own(a):
-        return pltpu.make_async_copy(
-            sources[a].at[:, columns(z * 2 + half(y))], landing(a, 0, y % 2), own_sem.at[a]
-        )
-
-    for a in range(4):
+        if a < 2:
+            dst = kv.at[a, 0, x, c, side, rows(odd)]
+        else:
+            dst = (q_out, n_out)[a - 2].at[0, rows(odd)]
+        return pltpu.make_async_copy(sources.at[a, :, columns(z * 2 + mine)], dst, own_sem.at[a])
+
+    def send_tiles(first):
+        for slot in range(NZ):
+            for turn in (1, 0) if slot else (1,):
+                for a in (first + 1, first):
+                    tile_out(a, slot, turn).start()
+
+    for a in (1, 0, 2, 3):
         tile_own(a).start()
-
-    def send_tiles(first):
-        tile_out(first, 0, 1).start()
-        tile_out(first + 1, 0, 1).start()
-
-        def start(slot, carry):
-            for turn in range(2):
-                tile_out(first, slot, turn).start()
-                tile_out(first + 1, slot, turn).start()
-            return carry
-
-        lax.fori_loop(1, NZ, start, 0)
-
     send_tiles(0)
 
-    def chunk(a, part, dx, core, g):
-        return kv.at[a, part, around(x, dx, NX), core, side if g == 0 else 1 - side]
+    def chunk(a, part, dx, g):
+        return kv.at[a, part, xs[dx % NX], c, side if g == 0 else 1 - side]
 
     def along_x(a, part, g, leg):
         way = far_way(a, part)
         dx, to = {LONG1: (0, way), LONG2: (-way, way), SHORT: (0, -way)}[leg]
-        ref = chunk(a, part, dx, c, g)
-        return remote(
-            ref, ref, x_send.at[a, part, g, leg], x_recv.at[a, part, g, leg],
-            device(z, around(x, to, NX), y, c),
-        )
-
-    def from_x(a, part, g, leg):
+        ref = chunk(a, part, dx, g)
+        return remote(ref, ref, x_send.at[a, g, leg], x_recv.at[a, part, g, leg], to_x[to])
+
+    def over_y(a, part, dx):
+        ref = chunk(a, part, dx, 0)
+        return remote(ref, ref, y_send.at[a, dx % NX], y_recv.at[a, part], to_y)
+
+    def got_y(a, part):
+        if x_first(a, part):
+            ref = kv.at[a, part, :, c, 1 - side]
+        else:
+            ref = chunk(a, part, 0, 1)
+        remote(ref, ref, y_send.at[a, 0], y_recv.at[a, part], to_y).wait_recv()
+
+    def pair(a, part):
+        ref = kv.at[a, part, :, c]
+        return remote(ref, ref, pair_send.at[0], pair_recv.at[0], to_core)
+
+    def entered(a, part):
+        if part == 0:
+            tile_own(a).wait()
+            ref = kv.at[a, 0, x, c, side, rows(1 - odd)]
+        else:
+            ref = chunk(a, part, 0, 0)
+        remote(ref, ref, tile_send.at[a, 1], tile_recv.at[a, part], to_y).wait_recv()
+
+    def got_x(a, part, g, leg):
         way = far_way(a, part)
-        dx, of = {LONG1: (-way, -way), LONG2: (-2 * way, -way), SHORT: (way, way)}[leg]
-        ref = chunk(a, part, dx, c, g)
-        return dx, remote(
-            ref, ref, x_send.at[a, part, g, leg], x_recv.at[a, part, g, leg],
-            device(z, around(x, of, NX), y, c),
-        )
-
-    def over_y(a, part, dx, g):
-        ref = chunk(a, part, dx, c, g)
-        return remote(
-            ref, ref, y_send.at[a, part, dx % NX], y_recv.at[a, part, dx % NX],
-            device(z, x, NY - 1 - y, c),
-        )
-
-    def pair(a, part, dx, g, core):
-        ref = chunk(a, part, dx, core, g)
-        return remote(
-            ref, ref, pair_send.at[a, part, g, dx % NX], pair_recv.at[a, part, g, dx % NX],
-            device(z, x, y, 1 - c),
-        )
-
-    def entered(a, part):
-        for turn in range(2):
-            if part == 0 and turn == 0:
-                tile_own(a).wait()
-            else:
-                tile_in(a, part, turn).wait_recv()
-
-    def got_x(a, part, g, leg):
-        dx, copy = from_x(a, part, g, leg)
-        copy.wait_recv()
+        dx = {LONG1: -way, LONG2: -2 * way, SHORT: way}[leg]
+        ref = chunk(a, part, dx, g)
+        remote(ref, ref, x_send.at[a, g, leg], x_recv.at[a, part, g, leg], to_y).wait_recv()
         if leg == LONG1:
             along_x(a, part, g, LONG2).start()
         if x_first(a, part):
-            over_y(a, part, dx, 0).start()
-        pair(a, part, dx, g, c).start()
+            over_y(a, part, dx).start()
 
     def stage_a(part):
         for a in (1, 0):
             entered(a, part)
-            over_y(a, part, 0, 0).start()
+            over_y(a, part, 0).start()
             along_x(a, part, 0, LONG1).start()
             along_x(a, part, 0, SHORT).start()
-            pair(a, part, 0, 0, c).start()
 
     def stage_b(part):
         for a in (1, 0):
             if not x_first(a, part):
-                over_y(a, part, 0, 1).wait_recv()
+                got_y(a, part)
                 along_x(a, part, 1, LONG1).start()
                 along_x(a, part, 1, SHORT).start()
-                pair(a, part, 0, 1, c).start()
         for a in (0, 1):
             got_x(a, part, 0, LONG1)
             got_x(a, part, 0, SHORT)
@@ -233,14 +222,10 @@
     def stage_d(part):
         for a in (1, 0):
             if x_first(a, part):
-                for dx in range(NX):
-                    over_y(a, part, dx, 1).wait_recv()
-                    pair(a, part, dx, 1, c).start()
+                got_y(a, part)
             else:
                 got_x(a, part, 1, LONG2)
-
-    def clear(a, i):
-        return pltpu.make_async_copy(zeros, cleared.at[a, pl.ds(i * 64, 64)], clear_sem.at[a, i])
+            pair(a, part).start()
 
     stages = (stage_a, stage_b, stage_c, stage_d)
     for time in range(NZ + len(stages) - 1):
@@ -251,40 +236,34 @@
             zeros[...] = jnp.zeros(zeros.shape, jnp.bfloat16)
             for a in range(2):
                 for i in range(NB // 64):
-                    clear(a, i).start()
+                    pltpu.make_async_copy(
+                        zeros, cleared.at[a, pl.ds(i * 64, 64)], clear_sem.at[0]
+                    ).start()
         if time == 4:
             send_tiles(2)
 
-    for a in range(2):
-        for i in range(NB // 64):
-            clear(a, i).wait()
+    pltpu.make_async_copy(cleared, cleared, clear_sem.at[0]).wait()
     for a in (2, 3):
         tile_own(a).wait()
     for a in range(4):
-        tile_out(a, 0, 1).wait_send()
-        if a >= 2:
-            tile_in(a, 0, 1).wait_recv()
-
-    def finish(slot, carry):
         for turn in range(2):
-            for a in range(4):
-                tile_out(a, slot, turn).wait_send()
-                if a >= 2:
-                    tile_in(a, slot, turn).wait_recv()
-        return carry
-
-    lax.fori_loop(1, NZ, finish, 0)
-    for part in range(NZ):
-        for a in range(2):
-            for g in sides(a, part):
+            tiles(a, turn).wait_send()
+            if a >= 2:
+                tiles(a, turn).wait_recv()
+    for a in range(2):
+        for g in range(2):
+            if count := part_count(a, g):
+                ref = kv.at[a, pl.ds(0, count), x, c, side]
                 for leg in range(3):
-                    along_x(a, part, g, leg).wait_send()
-            for dx in range(over_count(a, part)):
-                over_y(a, part, dx, 0).wait_send()
-            for g in range(2):
-                for dx in range(NX):
-                    pair(a, part, dx, g, c).wait_send()
-                    pair(a, part, dx, g, 1 - c).wait_recv()
+                    remote(ref, ref, x_send.at[a, g, leg], x_recv.at[a, 0, g, leg], to_y).wait_send()
+        for dx in range(NX):
+            if count := sum(dx < over_count(a, part) for part in range(NZ)):
+                ref = kv.at[a, pl.ds(0, count), x, c, side]
+                remote(ref, ref, y_send.at[a, dx], y_recv.at[a, 0], to_y).wait_send()
+    ref = kv.at[:, :, :, c]
+    remote(ref, ref, pair_send.at[0], pair_recv.at[0], to_core).wait_send()
+    ref = kv.at[:, :, :, 1 - c]
+    remote(ref, ref, pair_send.at[0], pair_recv.at[0], to_core).wait_recv()
 
 
 def attend_kernel(random_blocks, global_blocks, q, n, kv, cleared, att, dq, acc, global_sum):
@@ -383,12 +362,17 @@
 ):
     z, x, y, c = place()
     greet(z, x, y, c)
-    side = y // 2
+    side, odd = lax.div(y, 2), lax.rem(y, 2)
+    xs = [around(x, dx, NX) for dx in range(NX)]
+    other_y = beside(y)
+    to_x = {1: device(z, xs[1], y, c), -1: device(z, xs[-1], y, c)}
+    to_y, to_core = device(z, x, NY - 1 - y, c), device(z, x, y, 1 - c)
+    head = columns(z * 2 + half(y))
 
     def pair(a, part):
         return remote(
-            partial.at[a, part, :, 1 - c], sib.at[a, part],
-            pair_send.at[a, part], pair_recv.at[a, part], device(z, x, y, 1 - c),
+            partial.at[a, part, :, 1 - c], sib.at[a, part], pair_send.at[0], pair_recv.at[a, part],
+            to_core,
         )
 
     order = tuple(reversed(range(NZ)))
@@ -398,81 +382,26 @@
 
     outs = (dk_out, dv_out, att_out, dq_out)
 
-    def source(a, slot, row):
+    def source(a, slots, row):
         if a < 2:
-            return own.at[a, slot, x, side, rows(row)]
-        return (att, dq)[a - 2].at[slot, rows(row)]
+            return own.at[a, slots, x, side, rows(row)]
+        return (att, dq)[a - 2].at[slots, rows(row)]
 
     def tile_out(a, slot, turn):
-        tz, ty = (z + offset(slot) + NZ) % NZ, beside(y) if turn else y
         return remote(
-            source(a, slot, ty % 2), outs[a].at[:, columns(z * 2 + half(y))],
-            tile_send.at[a, turn, slot], tile_recv.at[a, turn, slot], device(tz, x, ty, c),
+            source(a, slot, 1 - odd if turn else odd), outs[a].at[:, head], tile_send.at[a, turn],
+            tile_recv.at[a, turn], device(around(z, offset(slot), NZ), x, other_y if turn else y, c),
         )
 
-    def tile_in(a, slot, turn):
-        fz, fy = (z - offset(slot) + NZ) % NZ, beside(y) if turn else y
+    def tiles(a, turn):
+        count = NZ - 1 + turn
         return remote(
-            source(a, slot, y % 2), outs[a].at[:, columns(fz * 2 + half(fy))],
-            tile_send.at[a, turn, slot], tile_recv.at[a, turn, slot], device(fz, x, fy, c),
+            source(a, pl.ds(0, count), 0), outs[a].at[:, pl.ds(0, count * DH)], tile_send.at[a, turn],
+            tile_recv.at[a, turn], to_y,
         )
 
     def tile_own(a):
-        return pltpu.make_async_copy(
-            source(a, 0, y % 2), outs[a].at[:, columns(z * 2 + half(y))], tile_sem.at[a]
-        )
-
-    for a in (2, 3):
-        tile_own(a).start()
-        tile_out(a, 0, 1).start()
-
-    def start(slot, carry):
-        for turn in range(2):
-            tile_out(2, slot, turn).start()
-            tile_out(3, slot, turn).start()
-        return carry
-
-    lax.fori_loop(1, NZ, start, 0)
-
-    def sum_up(a, part, dx, g, first, came):
-        xs, gs = around(x, dx, NX), side if g == 0 else 1 - side
-
-        def span(i, carry):
-            at = rows(i)
-            if first:
-                total = partial[a, part, xs, c, gs, at].astype(jnp.float32)
-                total += sib[a, part, xs, gs, at].astype(jnp.float32)
-            else:
-                total = own[a, part, xs, gs, at].astype(jnp.float32)
-            for ref in came:
-                total += ref[at].astype(jnp.float32)
-            own[a, part, xs, gs, at] = total.astype(jnp.bfloat16)
-            return carry
-
-        lax.fori_loop(0, 2, span, 0)
-
-    def chunk(a, part, dx, g):
-        return own.at[a, part, around(x, dx, NX), side if g == 0 else 1 - side]
-
-    def landed_x(a, part, g, leg):
-        return x_came.at[2 * a + g, part, leg]
-
-    def landed_y(a, part, dx):
-        return y_came.at[part, dx % NX if a == 0 else NX]
-
-    def along_x(a, part, g, leg):
-        way = far_way(a, part)
-        dx, to = {LONG1: (2 * way, way), LONG2: (way, way), SHORT: (-way, -way)}[leg]
-        return remote(
-            chunk(a, part, dx, g), landed_x(a, part, g, leg), x_send.at[a, part, g, leg],
-            x_recv.at[a, part, g, leg], device(z, around(x, to, NX), y, c),
-        )
-
-    def over_y(a, part, dx):
-        return remote(
-            chunk(a, part, dx, 1), landed_y(a, part, dx), y_send.at[a, part, dx % NX],
-            y_recv.at[a, part, dx % NX], device(z, x, NY - 1 - y, c),
-        )
+        return pltpu.make_async_copy(source(a, 0, odd), outs[a].at[:, head], tile_sem.at[a])
 
     def send_tiles(a, part):
         for turn in range(2):
@@ -480,6 +409,40 @@
                 tile_own(a).start()
             else:
                 tile_out(a, part, turn).start()
+
+    def sum_up(a, part, dx, g, first, came):
+        at_x, gs = xs[dx % NX], side if g == 0 else 1 - side
+        if first:
+            total = partial[a, part, at_x, c, gs].astype(jnp.float32)
+            total += sib[a, part, at_x, gs].astype(jnp.float32)
+        else:
+            total = own[a, part, at_x, gs].astype(jnp.float32)
+        for ref in came:
+            total += ref[...].astype(jnp.float32)
+        own[a, part, at_x, gs] = total.astype(jnp.bfloat16)
+
+    def chunk(a, part, dx, g):
+        return own.at[a, part, xs[dx % NX], side if g == 0 else 1 - side]
+
+    def landed_x(a, part, g, leg):
+        return x_came.at[2 * a + g, part, leg]
+
+    def landed_y(a, part, dx):
+        return y_came.at[part, dx % NX if a == 0 else NX]
+
+    def along_x(a, part, g, leg):
+        way = far_way(a, part)
+        dx, to = {LONG1: (2 * way, way), LONG2: (way, way), SHORT: (-way, -way)}[leg]
+        return remote(
+            chunk(a, part, dx, g), landed_x(a, part, g, leg), x_send.at[a, g, leg],
+            x_recv.at[a, part, g, leg], to_x[to],
+        )
+
+    def over_y(a, part, dx):
+        return remote(
+            chunk(a, part, dx, 1), landed_y(a, part, dx), y_send.at[a, dx % NX],
+            y_recv.at[a, part, dx % NX], to_y,
+        )
 
     def leg(a, part, g, dx, name, came):
         if x_first(a, part):
@@ -539,6 +502,10 @@
                 sum_up(a, part, 0, 0, False, [landed_y(a, part, 0)])
             send_tiles(a, part)
 
+    for part in order:
+        for a in (2, 3):
+            send_tiles(a, part)
+
     plan = ((after_y, 1), (begin, 0), (seconds, 2), (over, 3), (lasts, 4))
     for time in range(NZ + 4):
         for stage, late in plan:
@@ -547,25 +514,22 @@
 
     for a in range(4):
         tile_own(a).wait()
-        tile_out(a, 0, 1).wait_send()
-        tile_in(a, 0, 1).wait_recv()
-
-    def finish(slot, carry):
         for turn in range(2):
-            for a in range(4):
-                tile_out(a, slot, turn).wait_send()
-                tile_in(a, slot, turn).wait_recv()
-        return carry
-
-    lax.fori_loop(1, NZ, finish, 0)
-    for part in range(NZ):
-        for a in range(2):
-            pair(a, part).wait_send()
-            for g in sides(a, part):
+            tiles(a, turn).wait_send()
+            tiles(a, turn).wait_recv()
+    for a in range(2):
+        for g in range(2):
+            if count := part_count(a, g):
+                ref = own.at[a, pl.ds(0, count), x, side]
                 for name in range(3):
-                    along_x(a, part, g, name).wait_send()
-            for dx in range(over_count(a, part)):
-                over_y(a, part, dx).wait_send()
+                    remote(ref, ref, x_send.at[a, g, name], x_recv.at[a, 0, g, name], to_y).wait_send()
+        for dx in range(NX):
+            if count := sum(dx < over_count(a, part) for part in range(NZ)):
+                ref = own.at[a, pl.ds(0, count), x, side]
+                remote(ref, ref, y_send.at[a, dx], y_recv.at[a, 0, dx], to_y).wait_send()
+    remote(
+        partial.at[:, :, :, 1 - c], sib, pair_send.at[0], pair_recv.at[0, 0], to_core
+    ).wait_send()
 
 
 def write_kernel(*refs):
@@ -598,16 +562,17 @@
         out_shape=(
             bf16(NZ, SIDE, DH), bf16(NZ, SIDE, DH), bf16(*gathered), bf16(2, NB, BLK, DH)
         ),
-        in_specs=[ANY] * 4,
+        in_specs=[ANY],
         out_specs=(ANY, ANY, ANY, ANY),
         scratch_shapes=[
-            *copies(4, 2, NZ), DMA((4,)), *copies(2, NZ, 2, 3), *copies(2, NZ, NX),
-            *copies(2, NZ, 2, NX), pltpu.VMEM((64, BLK, DH), jnp.bfloat16), DMA((2, NB // 64)),
+            DMA((4, 2)), DMA((4, NZ)), DMA((4,)), DMA((2, 2, 3)), DMA((2, NZ, 2, 3)),
+            DMA((2, NX)), DMA((2, NZ)), *copies(1), pltpu.VMEM((64, BLK, DH), jnp.bfloat16), DMA((1,)),
         ],
+        cost_estimate=pl.CostEstimate(flops=8 * 10**10, bytes_accessed=1, transcendentals=0),
         compiler_params=pltpu.CompilerParams(
             collective_id=0, has_side_effects=True, vmem_limit_bytes=FETCH_MIB * 2**20
         ),
-    )(queries, keys, values, noise)
+    )(jnp.stack([keys, values, queries, noise]))
 
     att, dq, partial = pl.pallas_call(
         attend_kernel,
@@ -634,8 +599,8 @@
             pltpu.VMEM((2, NZ, NX, 2, SIDE, DH), jnp.bfloat16),
             pltpu.VMEM((4, NZ, 3, SIDE, DH), jnp.bfloat16),
             pltpu.VMEM((NZ, NX + 1, SIDE, DH), jnp.bfloat16),
-            *copies(2, NZ), *copies(2, NZ, 2, 3), *copies(2, NZ, NX),
-            *copies(4, 2, NZ), DMA((4,)),
+            DMA((1,)), DMA((2, NZ)), DMA((2, 2, 3)), DMA((2, NZ, 2, 3)), DMA((2, NX)),
+            DMA((2, NZ, NX)), *copies(4, 2), DMA((4,)),
         ],
         compiler_params=pltpu.CompilerParams(
             collective_id=1, has_side_effects=True, vmem_limit_bytes=RETURN_MIB * 2**20

time: 170 us -> 163 us (0.959)
  local copies, waits for them, and re-layouts: 5.5 us -> 0.01 us
  Pallas kernels: 164 us -> 161 us
  other arithmetic: 0 us -> 1.78 us
    unnamed x12 -> x4, local copies, waits for them, and re-layouts: 5.5 us -> 0.01 us
    pallas_call x1, Pallas kernels: 75.3 us -> 72.6 us  [shards(): pl.pallas_call(return_kernel, name='give_back', out_shape=(bf16(ROWS, HEA...]
    another operation x0 -> x1, other arithmetic: none -> 1.78 us  [shards(): jnp.stack([keys, values, queries, noise])]
where the time goes in v4:
time: 163 us
  Pallas kernels  161 us (99%)
  other arithmetic  1.78 us (1%)
    pallas_call x1, Pallas kernels, shards(): pl.pallas_call(fetch_kernel, name='fetch', out_shape=(bf16(NZ, SIDE, DH),...  76.1 us
    pallas_call x1, Pallas kernels, shards(): pl.pallas_call(return_kernel, name='give_back', out_shape=(bf16(ROWS, HEA...  72.6 us
    pallas_call x1, Pallas kernels, shards(): pl.pallas_call(attend_kernel, name='attend', out_shape=(bf16(QUERIES, BLK...  10.5 us

profile of v4, /device:TPU:8, one launch (start us, length us, event | category | flops | bytes accessed | tf_op | source)
XLA Modules:
  0.0 163.1 jit_solution(12204889317626928314)
XLA Ops:
  0.6 1.8 %pad_maximum_fusion.sources = bf16[4,128,2048]{2,1,0:T(8,128)(2,1)S(1)} fusion(bf16[1,128,2048]{2,1,0:T(8,128)(2,1)} %bitcast.18, bf16[1,128,2048]{2,1,0:T(8,128)(2,1)} %bitcast.19, bf16[1,128,2048]{2,1,0:T(8,128)(2,1)} %bitcast.20, bf16[1,128,2048]{2,1,0:T(8,128)(2,1)} %bitcast.21), kind=kLoop, calls=%fused_computation | loop fusion | flops 3145728 | bytes 4194304 | tf_op jit(solution)/shard_map/stack | solution.py:575
  2.4 0.0 copy-start
  2.4 0.0 copy-start.1
  2.4 76.1 %fetch.1 = (bf16[8,256,128]{2,1,0:T(8,128)(2,1)S(1)}, bf16[8,256,128]{2,1,0:T(8,128)(2,1)S(1)}, bf16[2,8,4,2,2,256,128]{6,5,4,3,2,1,0:T(8,128)(2,1)S(1)}, bf16[2,512,64,128]{3,2,1,0:T(8,128)(2,1)S(1)}) custom-call(bf16[4,128,2048]{2,1,0:T(8,128)(2,1)S(1)} %pad_maximum_fusion.sources), custom_call_target="tpu_custom_call" | custom-call | flops 80000000000 | bytes 1 | tf_op jit(solution)/shard_map/fetch/pallas_call | solution.py:559
  78.6 0.0 copy-done
  78.6 0.0 copy-done.1
  78.6 10.5 %attend.1 = (bf16[32,64,128]{2,1,0:T(8,128)(2,1)S(1)}, bf16[32,64,128]{2,1,0:T(8,128)(2,1)S(1)}, bf16[2,512,64,128]{3,2,1,0:T(8,128)(2,1)S(1)}) custom-call(s32[3,512]{1,0:T(4,128)S(1)} %bitcast.17, s32[2]{0:T(128)S(1)} %copy-done.1, bf16[32,64,128]{2,1,0:T(8,128)(2,1)S(1)} %bitcast.15, ...), custom_call_target="tpu_custom_call", output_to_operand_aliasing={{2}: (5, {})} | custom-call | tf_op jit(solution)/shard_map/attend/pallas_call | solution.py:577
  89.1 72.6 %give_back.1 = (bf16[128,2048]{1,0:T(8,128)(2,1)S(1)}, bf16[128,2048]{1,0:T(8,128)(2,1)S(1)}, bf16[128,2048]{1,0:T(8,128)(2,1)S(1)}, bf16[128,2048]{1,0:T(8,128)(2,1)S(1)}) custom-call(bf16[8,256,128]{2,1,0:T(8,128)(2,1)S(1)} %bitcast.13, bf16[8,256,128]{2,1,0:T(8,128)(2,1)S(1)} %bitcast.14, bf16[2,8,4,2,2,256,128]{6,5,4,3,2,1,0:T(8,128)(2,1)S(1)} %bitcast.11), custom_call_target="tpu_custom_call" | custom-call | tf_op jit(solution)/shard_map/give_back/pallas_call | solution.py:591
  161.7 1.3 write.1
Async XLA Ops:
  2.4 76.2 %copy-start = (s32[512,3]{0,1:T(4,128)S(1)}, s32[512,3]{0,1:T(4,128)}, u32[]{:S(2)}) copy-start(s32[512,3]{0,1:T(4,128)} %param.10) | copy-start | bytes 18436
  2.4 76.2 %copy-start.1 = (s32[2]{0:T(128)S(1)}, s32[2]{0:T(128)}, u32[]{:S(2)}) copy-start(s32[2]{0:T(128)} %global_blocks.1) | copy-start | bytes 28

commit v5 on v4

--- a/solution.py
+++ b/solution.py
@@ -18,7 +18,7 @@
 QUERIES = NZ * SIDE // BLK
 HEADS = 16
 ENTRIES = 8
-GROUP = 8
+GROUP = 16
 FETCH_MIB, ATTEND_MIB, RETURN_MIB = 4, 8, 26
 MESH = pl.DeviceIdType.MESH
 
@@ -142,15 +142,15 @@
             dst = (q_out, n_out)[a - 2].at[0, rows(odd)]
         return pltpu.make_async_copy(sources.at[a, :, columns(z * 2 + mine)], dst, own_sem.at[a])
 
-    def send_tiles(first):
-        for slot in range(NZ):
+    def send_tiles(first, slots):
+        for slot in slots:
             for turn in (1, 0) if slot else (1,):
                 for a in (first + 1, first):
                     tile_out(a, slot, turn).start()
 
     for a in (1, 0, 2, 3):
         tile_own(a).start()
-    send_tiles(0)
+    send_tiles(0, range(3))
 
     def chunk(a, part, dx, g):
         return kv.at[a, part, xs[dx % NX], c, side if g == 0 else 1 - side]
@@ -233,14 +233,16 @@
             if 0 <= time - late < NZ:
                 stage(time - late)
         if time == 0:
+            send_tiles(0, range(3, NZ))
+        if time == 2:
             zeros[...] = jnp.zeros(zeros.shape, jnp.bfloat16)
             for a in range(2):
                 for i in range(NB // 64):
                     pltpu.make_async_copy(
                         zeros, cleared.at[a, pl.ds(i * 64, 64)], clear_sem.at[0]
                     ).start()
-        if time == 4:
-            send_tiles(2)
+        if 3 <= time < 3 + NZ // 2:
+            send_tiles(2, (2 * time - 6, 2 * time - 5))
 
     pltpu.make_async_copy(cleared, cleared, clear_sem.at[0]).wait()
     for a in (2, 3):
@@ -502,15 +504,14 @@
                 sum_up(a, part, 0, 0, False, [landed_y(a, part, 0)])
             send_tiles(a, part)
 
-    for part in order:
-        for a in (2, 3):
-            send_tiles(a, part)
-
     plan = ((after_y, 1), (begin, 0), (seconds, 2), (over, 3), (lasts, 4))
     for time in range(NZ + 4):
         for stage, late in plan:
             if 0 <= time - late < NZ:
                 stage(order[time - late])
+        if time < NZ:
+            for a in (2, 3):
+                send_tiles(a, order[time])
 
     for a in range(4):
         tile_own(a).wait()

time: 163 us -> 160 us (0.982)
  Pallas kernels: 161 us -> 158 us
    pallas_call x1, Pallas kernels: 72.6 us -> 70.7 us  [shards(): pl.pallas_call(return_kernel, name='give_back', out_shape=(bf16(ROWS, HEA...]
where the time goes in v5:
time: 160 us
  Pallas kernels  158 us (99%)
  other arithmetic  1.78 us (1%)
    pallas_call x1, Pallas kernels, shards(): pl.pallas_call(fetch_kernel, name='fetch', out_shape=(bf16(NZ, SIDE, DH),...  76.6 us
    pallas_call x1, Pallas kernels, shards(): pl.pallas_call(return_kernel, name='give_back', out_shape=(bf16(ROWS, HEA...  70.7 us
    pallas_call x1, Pallas kernels, shards(): pl.pallas_call(attend_kernel, name='attend', out_shape=(bf16(QUERIES, BLK...  9.07 us

profile of v5, /device:TPU:8, one launch (start us, length us, event | category | flops | bytes accessed | tf_op | source)
XLA Modules:
  0.0 160.2 jit_solution(17105238763041701716)
XLA Ops:
  0.6 1.8 %pad_maximum_fusion.sources = bf16[4,128,2048]{2,1,0:T(8,128)(2,1)S(1)} fusion(bf16[1,128,2048]{2,1,0:T(8,128)(2,1)} %bitcast.18, bf16[1,128,2048]{2,1,0:T(8,128)(2,1)} %bitcast.19, bf16[1,128,2048]{2,1,0:T(8,128)(2,1)} %bitcast.20, bf16[1,128,2048]{2,1,0:T(8,128)(2,1)} %bitcast.21), kind=kLoop, calls=%fused_computation | loop fusion | flops 3145728 | bytes 4194304 | tf_op jit(solution)/shard_map/stack | solution.py:576
  2.4 0.0 copy-start
  2.4 0.0 copy-start.1
  2.4 76.6 %fetch.1 = (bf16[8,256,128]{2,1,0:T(8,128)(2,1)S(1)}, bf16[8,256,128]{2,1,0:T(8,128)(2,1)S(1)}, bf16[2,8,4,2,2,256,128]{6,5,4,3,2,1,0:T(8,128)(2,1)S(1)}, bf16[2,512,64,128]{3,2,1,0:T(8,128)(2,1)S(1)}) custom-call(bf16[4,128,2048]{2,1,0:T(8,128)(2,1)S(1)} %pad_maximum_fusion.sources), custom_call_target="tpu_custom_call" | custom-call | flops 80000000000 | bytes 1 | tf_op jit(solution)/shard_map/fetch/pallas_call | solution.py:560
  79.0 0.0 copy-done
  79.1 0.0 copy-done.1
  79.1 9.1 %attend.1 = (bf16[32,64,128]{2,1,0:T(8,128)(2,1)S(1)}, bf16[32,64,128]{2,1,0:T(8,128)(2,1)S(1)}, bf16[2,512,64,128]{3,2,1,0:T(8,128)(2,1)S(1)}) custom-call(s32[3,512]{1,0:T(4,128)S(1)} %bitcast.17, s32[2]{0:T(128)S(1)} %copy-done.1, bf16[32,64,128]{2,1,0:T(8,128)(2,1)S(1)} %bitcast.15, ...), custom_call_target="tpu_custom_call", output_to_operand_aliasing={{2}: (5, {})} | custom-call | tf_op jit(solution)/shard_map/attend/pallas_call | solution.py:578
  88.1 70.7 %give_back.1 = (bf16[128,2048]{1,0:T(8,128)(2,1)S(1)}, bf16[128,2048]{1,0:T(8,128)(2,1)S(1)}, bf16[128,2048]{1,0:T(8,128)(2,1)S(1)}, bf16[128,2048]{1,0:T(8,128)(2,1)S(1)}) custom-call(bf16[8,256,128]{2,1,0:T(8,128)(2,1)S(1)} %bitcast.13, bf16[8,256,128]{2,1,0:T(8,128)(2,1)S(1)} %bitcast.14, bf16[2,8,4,2,2,256,128]{6,5,4,3,2,1,0:T(8,128)(2,1)S(1)} %bitcast.11), custom_call_target="tpu_custom_call" | custom-call | tf_op jit(solution)/shard_map/give_back/pallas_call | solution.py:592
  158.8 1.3 write.1
Async XLA Ops:
  2.4 76.6 %copy-start = (s32[512,3]{0,1:T(4,128)S(1)}, s32[512,3]{0,1:T(4,128)}, u32[]{:S(2)}) copy-start(s32[512,3]{0,1:T(4,128)} %param.10) | copy-start | bytes 18436
  2.4 76.6 %copy-start.1 = (s32[2]{0:T(128)S(1)}, s32[2]{0:T(128)}, u32[]{:S(2)}) copy-start(s32[2]{0:T(128)} %global_blocks.1) | copy-start | bytes 28
